TPU v7x, 32 devices: a whole 2x2x4 slice. The times are simulated.
32 devices in a mesh: parts: 2 (over y), row: 2 (over core), col: 8 (over z, x).
Axes of the slice: x: 2, y: 2, z: 4, core: 2. Of those that a mesh axis runs over, the one named last changes fastest.
Arguments:
- sigma_anc: float32 [24576, 12288], P(('parts', 'col'), 'row'), parts along dimension 0, may hold values from -20 to 20, as said below
- factor_rows: float32 [4, 12288, 512], P('parts', ('row', 'col')), parts along dimension 0, may hold values from -0.0546875 to 0.0546875
- diag_inverse: float32 [4, 512, 512], P('parts'), parts along dimension 0, may hold values from -8 to 8, as said below
- row_pattern: int32 [4, 96], P('parts'), parts along dimension 0, may hold values 0 or 1
- anc_pattern: int32 [192, 96], P('parts'), parts along dimension 0, may hold values 0 or 1
Outputs:
- sigma_cross: float32 [4, 12288, 512], P('parts', 'col'), parts along dimension 0
- sigma_diag: float32 [4, 512, 512], P('parts'), parts along dimension 0
There are 2 independent parts, one for each index of `parts`. A program takes and returns all parts, laid end to end along the dimension named above; each array names one. Nothing has to cross between parts.
Inputs may be any that keep to these rules, and one draw needn't show every extreme that they name: `sigma_anc`: symmetric. `diag_inverse`: each supernode's block is lower triangular.
All inputs are finite; a program needn't handle non-finite values.
Results may differ from a plain program's by a relative error of at most 0.000071.
Values sent between devices are 32-bit elements; how exact they have to be, the bound alone decides.
No kernel may reach another device: no remote copies, remote signals or barrier semaphores. Data moves between devices by JAX's collectives and lax.ppermute only.
A program may use at most 448 MiB of HBM per device.

v0:
```python
import jax
import jax.numpy as jnp
from jax import lax
from jax.sharding import PartitionSpec as P

BLK = 128


def broadcast(value, axis, source):
    kept = jnp.where(lax.axis_index(axis) == source, value, 0).astype(value.dtype)
    return lax.psum(kept, axis)


def on_device(sigma_anc, factor_rows, diag_inverse, row_pattern, anc_pattern):
    high = lax.Precision.HIGHEST
    nrow = lax.axis_size("row")
    ncol = lax.axis_size("col")
    row_idx = lax.axis_index("row")
    col_idx = lax.axis_index("col")
    own_rows = factor_rows.shape[1]
    grid_rows = sigma_anc.shape[0]
    grid_cols = sigma_anc.shape[1]
    own_start = (row_idx * ncol + col_idx) * own_rows
    row_mask = jnp.repeat(row_pattern.astype(jnp.float32), BLK, axis=1)
    local_mask = lax.dynamic_slice_in_dim(row_mask, own_start, own_rows, 1)
    lower = factor_rows * local_mask[:, :, None]
    anc_rows = jnp.repeat(anc_pattern.astype(jnp.float32), BLK, axis=0)
    anc_rows = lax.dynamic_slice_in_dim(anc_rows, col_idx * grid_rows, grid_rows, 0)
    anc_full = jnp.repeat(anc_rows, BLK, axis=1)
    block_mask = lax.dynamic_slice_in_dim(anc_full, row_idx * grid_cols, grid_cols, 1)
    kept = sigma_anc * block_mask
    window = col_idx * grid_rows - row_idx * grid_cols
    piece = lax.all_gather(lower, "col", axis=1, tiled=True)
    count = piece.shape[1]
    scaled_piece = jnp.einsum("sgb,sbc->sgc", piece, diag_inverse, precision=high)
    total = jnp.einsum("fg,sgc->sfc", kept, scaled_piece, precision=high)
    margin = jnp.zeros((scaled_piece.shape[0], grid_rows, scaled_piece.shape[2]), jnp.float32)
    padded = jnp.concatenate([margin, scaled_piece, margin], axis=1)
    offset = jnp.clip(window + grid_rows, 0, count + grid_rows)
    captured = lax.dynamic_slice_in_dim(padded, offset, grid_rows, 1)
    sigma_cross = -lax.psum(total, "row")
    owner = col_idx // (ncol // nrow)
    shared = broadcast(captured, "row", owner)
    square = jnp.einsum("sbc,sbd->scd", diag_inverse, diag_inverse, precision=high)
    term = jnp.einsum("sfc,sfd->scd", shared, sigma_cross, precision=high)
    total_term = lax.psum(term, "col")
    sigma_diag = square - total_term
    return (sigma_cross, sigma_diag)


def solution(mesh):
    in_specs = (
        P(("parts", "col"), "row"),
        P("parts", ("row", "col"), None),
        P("parts", None, None),
        P("parts", None),
        P("parts", None),
    )
    out_specs = (P("parts", "col", None), P("parts", None, None))
    return jax.shard_map(
        on_device, mesh=mesh, in_specs=in_specs, out_specs=out_specs, check_vma=False
    )
```

profile of v0, /device:TPU:1, one launch (start us, length us, event | category | flops | bytes accessed | tf_op | source)
XLA Modules:
  0.0 990.9 jit_solution(16391322959564897267)
XLA Ops:
  7.2 0.0 copy-start
  7.2 0.0 copy-start.1
  7.2 0.0 all-gather.2.cloned.1.call-start
  7.2 0.8 convert_element_type.8
  8.1 0.1 broadcast_bitcast_fusion
  8.1 0.1 copy.21
  8.3 3.8 broadcast_multiply_fusion
  12.1 0.0 all-gather.2.cloned.1.call-update
  12.1 0.0 all-reduce.6.cloned.1.call-start
  12.2 0.0 copy-done.1
  12.2 0.4 broadcast_in_dim.16
  12.6 0.1 constant_dynamic-slice_fusion
  12.7 24.6 %broadcast_in_dim.17 = f32[1536,96,128]{2,1,0:T(8,128)} broadcast(f32[1536,96]{1,0:T(8,128)S(1)} %constant_dynamic-slice_fusion), dimensions={0,1} | broadcast | bytes 76087296 | tf_op jit(solution)/shard_map/broadcast_in_dim | solution.py:29
  37.3 83.5 %copy.20 = f32[192,8,96,128]{3,1,2,0:T(8,128)} copy(f32[192,8,96,128]{3,2,1,0:T(8,128)} %bitcast.5) | data formatting | bytes 150994944
  120.8 374.0 %all-gather.2.cloned.1.call-done = f32[2,6144,512]{2,1,0:T(8,128)} async-done(((f32[2,768,512]{2,1,0:T(8,128)}), f32[2,6144,512]{2,1,0:T(8,128)}) %all-gather.2.cloned.1.call-update) | async-done | bytes 25165840 | tf_op jit(solution)/shard_map/all_gather | solution.py:33
  494.8 0.0 copy-done
  494.8 45.4 %fusion.13 = f32[2,6144,512]{2,1,0:T(8,128)} fusion(f32[2,6144,512]{2,1,0:T(8,128)} %all-gather.2.cloned.1.call-done, f32[2,512,512]{2,1,0:T(8,128)S(1)} %copy-done), kind=kOutput, calls=%fused_computation.21 | convolution fusion | flops 38654705664 | bytes 52428800 | tf_op jit(solution)/shard_map/sgb,sbc->sgc/dot_general | solution.py:35
  540.2 252.9 %fusion.7 = f32[2,1536,512]{1,2,0:T(8,128)} fusion(f32[2,6144,512]{2,1,0:T(8,128)} %fusion.13, f32[1536,6144]{1,0:T(8,128)} %param.5, f32[1536,12288]{1,0:T(8,128)} %bitcast.25, s32[]{:T(128)S(6)} %select_n.25), kind=kOutput, calls=%fused_computation.11 | convolution fusion | flops 115973554176 | bytes 106954752 | tf_op jit(solution)/shard_map/fg,sgc->sfc/dot_general | solution.py:36
  793.0 0.8 broadcast_in_dim.18
  793.8 7.3 fusion.6
  801.1 0.0 all-reduce.6.cloned.1.call-update
  801.1 0.0 all-reduce.4.cloned.1.call-start
  801.2 50.8 %all-reduce.6.cloned.1.call-done = (f32[2,1536,512]{1,2,0:T(8,128)}, f32[2,1536,512]{2,1,0:T(8,128)}) async-done(((f32[2,1536,512]{1,2,0:T(8,128)}, f32[2,1536,512]{2,1,0:T(8,128)}), (f32[2,1536,512]{1,2,0:T(8,128)}, f32[2,1536,512]{2,1,0:T(8,128)})) %all-reduce.6.cloned.1.call-update) | async-done | bytes 12582928 | tf_op jit(solution)/shard_map/psum | solution.py:41
  852.0 23.7 %fusion.11 = f32[2,512,512]{2,1,0:T(8,128)} fusion(f32[2,1536,512]{2,1,0:T(8,128)} %get-tuple-element.5, f32[2,1536,512]{1,2,0:T(8,128)} %get-tuple-element.4), kind=kOutput, calls=%fused_computation.19 | convolution fusion | flops 9665249280 | bytes 14680064 | tf_op jit(solution)/shard_map/sfc,sfd->scd/dot_general | solution.py:45
  875.7 0.0 all-reduce.4.cloned.1.call-update
  875.7 6.1 neg.3
  881.8 6.9 copy.11
  888.7 89.6 %all-reduce.4.cloned.1.call-done = f32[2,512,512]{2,1,0:T(8,128)} async-done(((f32[2,512,512]{2,1,0:T(8,128)}), f32[2,512,512]{2,1,0:T(8,128)}) %all-reduce.4.cloned.1.call-update) | async-done | bytes 2097168 | tf_op jit(solution)/shard_map/psum | solution.py:46
  978.3 5.9 convolution_subtract_fusion
  (2 shorter events, 0.0 us)
Async XLA Ops:
  7.2 487.6 %copy-start = (f32[2,512,512]{2,1,0:T(8,128)S(1)}, f32[2,512,512]{2,1,0:T(8,128)}, u32[]{:S(2)}) copy-start(f32[2,512,512]{2,1,0:T(8,128)} %param.7) | copy-start | bytes 6291460
  7.2 5.0 copy-start.1
  7.2 487.6 %all-gather.2.cloned.1.call-start = ((), (), s32[]{:S(2)}) async-start(), calls=%async_computation | async-start | bytes 28311552 | tf_op jit(solution)/shard_map/all_gather | solution.py:33
  12.1 839.9 %all-reduce.6.cloned.1.call-start = ((), (), s32[]{:S(2)}) async-start(), calls=%async_computation.2 | async-start | bytes 25165824 | tf_op jit(solution)/shard_map/psum | solution.py:41
  801.1 177.2 %all-reduce.4.cloned.1.call-start = ((), (), s32[]{:S(2)}) async-start(), calls=%async_computation.1 | async-start | bytes 4194304 | tf_op jit(solution)/shard_map/psum | solution.py:46
Sparse Core Ops, SparseCore 0:
  12.2 482.5 all-gather.1
  801.2 50.7 all-reduce.5
  875.9 102.4 all-reduce.3
where the time goes:
time: 1000 us; the launch traced here: 991 us
  waiting for transfers between devices  514 us (51%)
  matrix products  328 us (33%)
  local copies, waits for them, and re-layouts  116 us (12%)
  other arithmetic  18 us (2%)
  between operations  14 us (1%)
    all_gather x1, waiting for transfers between devices, on_device(): piece = lax.all_gather(lower, 'col', axis=1, tiled=True)  374 us
    dot_general x1, matrix products, on_device(): total = jnp.einsum('fg,sgc->sfc', kept, scaled_piece, precision=high)  253 us
    unnamed x8, local copies, waits for them, and re-layouts  90.6 us
    psum x1, waiting for transfers between devices, on_device(): total_term = lax.psum(term, 'col')  89.6 us
    psum x1, waiting for transfers between devices, on_device(): sigma_cross = -lax.psum(total, 'row')  50.8 us
    dot_general x1, matrix products, on_device(): jnp.einsum('sgb,sbc->sgc', piece, diag_inverse, precision=high)  45.4 us
    broadcast_in_dim x1, local copies, waits for them, and re-layouts, on_device(): anc_full = jnp.repeat(anc_rows, BLK, axis=1)  24.6 us
    dot_general x1, matrix products, on_device(): term = jnp.einsum('sfc,sfd->scd', shared, sigma_cross, precision=high)  23.7 us
  transfers between devices with their start and end apart: 3, of which 3 were waited for; matrix products, arithmetic and copies ran while one was open for 12% of the time, Pallas kernels for 0%

commit v1 on v0

v1 whole, which is shorter than its diff:
```python
import functools

import jax
import jax.numpy as jnp
from jax import lax
from jax.experimental import pallas as pl
from jax.experimental.pallas import tpu as pltpu
from jax.sharding import PartitionSpec as P

BLK = 128
HIGH = lax.Precision.HIGH
HIGHEST = lax.Precision.HIGHEST


def _accumulate_body(n, row_step, ncols_blk, has_acc, tab, mask, *refs):
    pieces, refs = refs[:n], refs[n:]
    a_ref = refs[0]
    acc_ref = refs[1] if has_acc else None
    out_ref, u_ref = refs[-2:]
    depth = pieces[0].shape[0]
    t = pl.program_id(0)

    @pl.when(t == 0)
    def _():
        if has_acc:
            out_ref[...] = acc_ref[...]
        else:
            out_ref[...] = jnp.zeros_like(out_ref)

    for k, piece in enumerate(pieces):

        @pl.when(t == k)
        def _(piece=piece):
            v = piece[...]
            hi = v.astype(jnp.bfloat16)
            u_ref[0:depth, :] = hi
            u_ref[depth : 2 * depth, :] = (v - hi.astype(jnp.float32)).astype(jnp.bfloat16)
            u_ref[2 * depth : 3 * depth, :] = hi

    per = depth // BLK
    col0 = tab[t] * per
    lane = lax.broadcasted_iota(jnp.int32, (1, depth), 1) // BLK
    for m in range(a_ref.shape[0] // row_step):
        rows = []
        for b in range(row_step // BLK):
            blk = m * (row_step // BLK) + b
            keep = jnp.zeros((1, depth), jnp.float32)
            for j in range(per):
                kept = mask[blk * ncols_blk + col0 + j].astype(jnp.float32)
                keep = jnp.where(lane == j, kept, keep)
            rows.append(a_ref[blk * BLK : (blk + 1) * BLK, :] * keep)
        a = jnp.concatenate(rows, axis=0)
        hi = a.astype(jnp.bfloat16)
        lo = (a - hi.astype(jnp.float32)).astype(jnp.bfloat16)
        lhs = jnp.concatenate([hi, hi, lo], axis=1)
        at = slice(m * row_step, (m + 1) * row_step)
        out_ref[at, :] += jnp.dot(lhs, u_ref[...], preferred_element_type=jnp.float32)


def accumulate(acc, sigma, mask, table, pieces):
    nrows, ncols = sigma.shape
    depth, width = pieces[0].shape
    n = len(pieces)
    row_step = next(s for s in (512, 256, 128) if nrows % s == 0)
    whole = lambda shape: pl.BlockSpec(shape, lambda t, *_: (0, 0), pipeline_mode=pl.Buffered(1))
    in_specs = [whole(p.shape) for p in pieces]
    in_specs.append(pl.BlockSpec((nrows, depth), lambda t, tab, mask: (0, tab[t])))
    args = [*pieces, sigma]
    if acc is not None:
        in_specs.append(whole(acc.shape))
        args.append(acc)
    return pl.pallas_call(
        functools.partial(_accumulate_body, n, row_step, ncols // BLK, acc is not None),
        grid_spec=pltpu.PrefetchScalarGridSpec(
            num_scalar_prefetch=2,
            grid=(n,),
            in_specs=in_specs,
            out_specs=whole((nrows, width)),
            scratch_shapes=[pltpu.VMEM((3 * depth, width), jnp.bfloat16)],
        ),
        out_shape=jax.ShapeDtypeStruct((nrows, width), jnp.float32),
        compiler_params=pltpu.CompilerParams(
            dimension_semantics=("arbitrary",), vmem_limit_bytes=48 * 2**20
        ),
        cost_estimate=pl.CostEstimate(
            flops=6 * n * depth * nrows * width,
            bytes_accessed=4 * (n * depth * nrows + n * depth * width + 2 * nrows * width),
            transcendentals=0,
        ),
    )(jnp.stack(table), mask, *args)


def _negate_body(acc_ref, got_ref, *refs):
    refs[-1][0] = -(acc_ref[...] + got_ref[...])


def negate_into(full, acc, got, shape, s, at):
    nrows, width = acc.shape
    step = nrows // 3
    tile = pl.BlockSpec((step, width), lambda i: (i, 0))
    in_specs, args, aliases = [tile, tile], [acc, got], {}
    if full is not None:
        in_specs.append(pl.BlockSpec(memory_space=pl.ANY))
        args.append(full)
        aliases = {2: 0}
    return pl.pallas_call(
        _negate_body,
        grid=(3,),
        in_specs=in_specs,
        out_specs=pl.BlockSpec((1, step, width), lambda i: (s, i, at // width)),
        out_shape=jax.ShapeDtypeStruct(shape, jnp.float32),
        input_output_aliases=aliases,
        compiler_params=pltpu.CompilerParams(vmem_limit_bytes=32 * 2**20),
        cost_estimate=pl.CostEstimate(
            flops=2 * nrows * width, bytes_accessed=12 * nrows * width, transcendentals=0
        ),
    )(*args)


def after(value, *deps):
    return lax.optimization_barrier((value, *deps))[0]


def grid_path(sigma_anc, factor_rows, diag_inverse, row_pattern, anc_pattern):
    ncol = lax.axis_size("col")
    r = lax.axis_index("row")
    c = lax.axis_index("col")
    z, x = c // 2, c % 2
    ns, own_rows, width = factor_rows.shape
    grid_rows, grid_cols = sigma_anc.shape

    mesh_pairs = lambda f, who: [(f(i), i) for i in range(ncol) if i // 2 in who]
    every, ends, mids = (0, 1, 2, 3), (0, 3), (1, 2)
    inner = lambda i: i + 2 if i < ncol // 2 else i - 2

    def recv(frm, v, who=every):
        return lax.ppermute(v, "col", mesh_pairs(frm, who))

    ox = lambda i: i ^ 1
    za = lambda i: i ^ 2
    zb = lambda i: i ^ 4

    row_mask = jnp.repeat(row_pattern.astype(jnp.float32), BLK, axis=1)
    local = lax.dynamic_slice_in_dim(row_mask, (r * ncol + c) * own_rows, own_rows, 1)
    lower = factor_rows * local[:, :, None]
    scale = lambda s, at, w: jnp.dot(lower[s], diag_inverse[s][:, at : at + w], precision=HIGH)

    mask = lax.dynamic_slice(
        anc_pattern,
        (c * (grid_rows // BLK), r * (grid_cols // BLK)),
        (grid_rows // BLK, grid_cols // BLK),
    ).reshape(-1)
    planes = (z, z ^ 1, jnp.where(z < 2, 2, 1), jnp.where(z < 2, 3, 0))
    near = [2 * p + x for p in planes]
    far = [2 * p + 1 - x for p in planes]

    def add(acc, *terms):
        return accumulate(acc, sigma_anc, mask, [i for i, _ in terms], [p for _, p in terms])

    def tdot(a, b, precision):
        dims = (((0,), (0,)), ((), ()))
        return lax.dot_general(a, b, dims, precision=precision)

    a0, b0 = lax.optimization_barrier((scale(0, 0, width), scale(1, 0, width)))
    a1, ax0, am = recv(za, a0), recv(ox, a0), recv(inner, a0, mids)
    b1, bx0 = recv(za, b0), recv(ox, b0)
    acc_a = add(None, (near[0], a0))
    acc_b = add(None, (near[0], b0))
    bm = recv(inner, after(b0, am), mids)
    square = jnp.concatenate([tdot(d, d, HIGHEST) for d in (diag_inverse[0], diag_inverse[1])])
    a1, ax0, am, b1, bx0, bm, acc_a, acc_b, square = lax.optimization_barrier(
        (a1, ax0, am, b1, bx0, bm, acc_a, acc_b, square)
    )
    ae, an, ax1 = recv(inner, am, ends), recv(inner, a1, mids), recv(ox, a1)
    be, bn = recv(inner, bm, ends), recv(inner, b1, mids)
    acc_a = add(acc_a, (far[0], ax0), (near[1], a1))
    acc_b = add(acc_b, (far[0], bx0), (near[1], b1))
    a2 = am + ae
    ax2 = recv(ox, after(a2, acc_a, acc_b))
    ax1, ax2, an, bn, a2, be, acc_a, acc_b = lax.optimization_barrier(
        (ax1, ax2, an, bn, a2, be, acc_a, acc_b)
    )
    b2 = bm + be
    af, bf, bx2 = recv(inner, an, ends), recv(inner, bn, ends), recv(ox, b2)
    acc_a = add(acc_a, (far[1], ax1), (near[2], a2))
    acc_b = add(acc_b, (near[2], b2))
    a3 = an + af
    ax3 = recv(ox, after(a3, acc_a, acc_b))
    acc_a = add(acc_a, (near[3], a3), (far[2], ax2))
    bf, bn, ax3, bx2, bx0, acc_a, acc_b = lax.optimization_barrier(
        (bf, bn, ax3, bx2, bx0, acc_a, acc_b)
    )
    b3 = bn + bf
    bx1, bx3 = recv(za, bx0), recv(ox, b3)
    acc_a = add(acc_a, (far[3], after(ax3, b3)))

    own_r = lambda i: i // (ncol // 2)
    holder = lambda i: own_r(i) * ncol + i
    other = lambda i: (1 - own_r(i)) * ncol + i
    is_holder = r == c // (ncol // 2)
    wanted = c % (ncol // 2)

    def recv_holder(frm, v):
        pairs = [(holder(frm(i)), holder(i)) for i in range(ncol)]
        return lax.ppermute(v, ("row", "col"), pairs)

    def choose(p0, p1, p2, p3):
        first = jnp.where(wanted == planes[0], p0, p1)
        second = jnp.where(wanted == planes[2], p2, p3)
        return jnp.where((wanted == planes[0]) | (wanted == planes[1]), first, second)

    def total(term, parts, work):
        size = term.shape[0] // parts // 8 * 8
        cuts = [i * size for i in range(parts)] + [term.shape[0]]
        ways = [ox, za, zb]
        values = [term[cuts[k] : cuts[k + 1]] for k in range(parts)]
        for step in range(3):
            values = [v + recv_holder(ways[(k + step) % 3], v) for k, v in enumerate(values)]
            if step < len(work):
                values = [after(v, work[step]) for v in values]
        return jnp.concatenate(values)

    def local_term(acc, got, same, cros):
        same, cros = choose(*same), choose(*cros)
        cross = -(acc + got)
        out_same = lax.dynamic_slice_in_dim(cross, x * own_rows, own_rows, 0)
        out_cros = lax.dynamic_slice_in_dim(cross, (1 - x) * own_rows, own_rows, 0)
        return tdot(same, out_same, HIGH) + tdot(cros, out_cros, HIGH)

    swap = lambda v: lax.ppermute(v, "row", [(0, 1), (1, 0)])
    shape = (ns, grid_rows, width)
    got_a = swap(acc_a)
    acc_b = add(acc_b, (near[3], after(b3, got_a)), (far[2], bx2))
    got_a = after(got_a, acc_b)
    term_a = local_term(acc_a, got_a, (a0, a1, a2, a3), (ax0, ax1, ax2, ax3))
    acc_b = add(acc_b, (far[1], bx1), (far[3], after(bx3, term_a)))
    got_b = swap(acc_b)
    term_b = local_term(acc_b, got_b, (b0, b1, b2, b3), (bx0, bx1, bx2, bx3))
    half = negate_into(None, acc_a, got_a, shape, 0, 0)
    full = negate_into(half, acc_b, got_b, shape, 1, 0)
    term = total(jnp.concatenate([term_a, term_b]), 3, (half, full))
    pairs = [(holder(i), other(i)) for i in range(ncol)]
    term = jnp.where(is_holder, term, lax.ppermute(term, ("row", "col"), pairs))
    return full, (square - term).reshape(diag_inverse.shape)


def plain_path(sigma_anc, factor_rows, diag_inverse, row_pattern, anc_pattern):
    nrow = lax.axis_size("row")
    ncol = lax.axis_size("col")
    r = lax.axis_index("row")
    c = lax.axis_index("col")
    own_rows = factor_rows.shape[1]
    grid_rows, grid_cols = sigma_anc.shape
    row_mask = jnp.repeat(row_pattern.astype(jnp.float32), BLK, axis=1)
    local = lax.dynamic_slice_in_dim(row_mask, (r * ncol + c) * own_rows, own_rows, 1)
    lower = factor_rows * local[:, :, None]
    scaled = jnp.einsum("sgb,sbc->sgc", lower, diag_inverse, precision=HIGHEST)
    piece = lax.all_gather(scaled, "col", axis=1, tiled=True)
    anc = jnp.repeat(anc_pattern.astype(jnp.float32), BLK, axis=0)
    anc = lax.dynamic_slice_in_dim(anc, c * grid_rows, grid_rows, 0)
    anc = jnp.repeat(anc, BLK, axis=1)
    anc = lax.dynamic_slice_in_dim(anc, r * grid_cols, grid_cols, 1)
    total = jnp.einsum("fg,sgc->sfc", sigma_anc * anc, piece, precision=HIGHEST)
    cross = -lax.psum(total, "row")
    half = c // (ncol // nrow)
    start = (c % (ncol // nrow)) * grid_rows
    mine = lax.dynamic_slice_in_dim(piece, start, grid_rows, 1)
    mine = jnp.where(r == half, mine, 0.0)
    term = jnp.einsum("sfc,sfd->scd", mine, cross, precision=HIGHEST)
    term = lax.psum(term, ("row", "col"))
    square = jnp.einsum("sbc,sbd->scd", diag_inverse, diag_inverse, precision=HIGHEST)
    return cross, square - term


def on_device(sigma_anc, factor_rows, diag_inverse, row_pattern, anc_pattern):
    own_rows, ncol = factor_rows.shape[1], lax.axis_size("col")
    fits = (
        ncol == 8
        and lax.axis_size("row") == 2
        and own_rows % BLK == 0
        and factor_rows.shape[0] == 2
        and sigma_anc.shape[0] % (3 * BLK) == 0
    )
    path = grid_path if fits else plain_path
    return path(sigma_anc, factor_rows, diag_inverse, row_pattern, anc_pattern)


def solution(mesh):
    in_specs = (
        P(("parts", "col"), "row"),
        P("parts", ("row", "col"), None),
        P("parts", None, None),
        P("parts", None),
        P("parts", None),
    )
    out_specs = (P("parts", "col", None), P("parts", None, None))
    return jax.shard_map(
        on_device, mesh=mesh, in_specs=in_specs, out_specs=out_specs, check_vma=False
    )
```

time: 1000 us -> 387 us (0.39)
  waiting for transfers between devices: 514 us -> 162 us
  matrix products: 328 us -> 19.6 us
  Pallas kernels: 0 us -> 123 us
  local copies, waits for them, and re-layouts: 116 us -> 11.8 us
  starting transfers between devices: 0.12 us -> 39.9 us
  between operations: 14 us -> 1.56 us
    all_gather x1 -> x0, waiting for transfers between devices: 374 us -> none  [on_device(): piece = lax.all_gather(lower, 'col', axis=1, tiled=True)]
    dot_general x4 -> x8, matrix products: 328 us -> 19.6 us  [the longest x6 16.6 us: tdot(): return lax.dot_general(a, b, dims, precision=precision)]
    ppermute x0 -> x30, waiting for transfers between devices: none -> 162 us  [the longest x18 102 us: recv(): return lax.ppermute(v, 'col', mesh_pairs(frm, who))]
    psum x2 -> x0, waiting for transfers between devices: 140 us -> none  [the longest x1 89.6 us: on_device(): total_term = lax.psum(term, 'col')]
    pallas_call x0 -> x12, Pallas kernels: none -> 123 us  [the longest x10 116 us: accumulate(): pl.pallas_call(functools.partial(_accumulate_body, n, row_step, ncols //...]
    unnamed x8 -> x56, local copies, waits for them, and re-layouts: 90.6 us -> 10.8 us
    ppermute x0 -> x30, starting transfers between devices: none -> 39.9 us  [the longest x18 25.6 us: recv(): return lax.ppermute(v, 'col', mesh_pairs(frm, who))]
    broadcast_in_dim x3 -> x0, local copies, waits for them, and re-layouts: 25.8 us -> none  [the longest x1 24.6 us: on_device(): anc_full = jnp.repeat(anc_rows, BLK, axis=1)]
  transfers between devices with their start and end apart: 3 -> 30, of which waited for: 3 -> 13; matrix products, arithmetic and copies ran while one was open for 12% -> 8% of each run, Pallas kernels for 0% -> 26%
where the time goes in v1:
time: 387 us; the launch traced here: 383 us
  waiting for transfers between devices  162 us (42%)
  Pallas kernels  123 us (32%)
  starting transfers between devices  39.9 us (10%)
  other arithmetic  26.3 us (7%)
  matrix products  19.6 us (5%)
  local copies, waits for them, and re-layouts  11.8 us (3%)
    pallas_call x10, Pallas kernels, accumulate(): pl.pallas_call(functools.partial(_accumulate_body, n, row_step, ncols //...  116 us
    ppermute x18, waiting for transfers between devices, recv(): return lax.ppermute(v, 'col', mesh_pairs(frm, who))  102 us
    ppermute x1, waiting for transfers between devices, grid_path(): term = jnp.where(is_holder, term, lax.ppermute(term, ('row', 'col'), pairs))  54.5 us
    ppermute x18, starting transfers between devices, recv(): return lax.ppermute(v, 'col', mesh_pairs(frm, who))  25.6 us
    dot_general x6, matrix products, tdot(): return lax.dot_general(a, b, dims, precision=precision)  16.6 us
    unnamed x56, local copies, waits for them, and re-layouts  10.8 us
  transfers between devices with their start and end apart: 30, of which 13 were waited for; matrix products, arithmetic and copies ran while one was open for 8% of the time, Pallas kernels for 26%

profile of v1, /device:TPU:1, one launch (start us, length us, event | category | flops | bytes accessed | tf_op | source)
XLA Modules:
  0.0 383.5 jit_solution(17484118718486552563)
XLA Ops:
  1.5 2.3 broadcast_multiply_fusion
  8.9 3.6 collective-permute-start
  14.0 2.3 collective-permute-start.5
  17.2 3.5 fusion.32
  24.1 6.8 %shard_map.68.refs_3_ = f32[1536,512]{1,0:T(8,128)S(1)} custom-call(s32[1]{0:T(128)} %bitcast.6.tab, s32[576]{0:T(1024)S(1)} %reshape.14.mask, f32[768,512]{1,0:T(8,128)S(1)} %fusion.1.refs_0_, f32[1536,6144]{1,0:T(8,128)} %refs_2_.11), custom_call_target="tpu_custom_call" | custom-call | flops 3623878656 | bytes 12582912 | tf_op jit(solution)/shard_map/pallas_call | solution.py:72
  32.6 6.8 %shard_map.69.refs_3_ = f32[1536,512]{1,0:T(8,128)S(1)} custom-call(s32[1]{0:T(128)} %bitcast.6.tab, s32[576]{0:T(1024)S(1)} %reshape.14.mask, f32[768,512]{1,0:T(8,128)S(1)} %fusion.refs_0_, f32[1536,6144]{1,0:T(8,128)} %refs_2_.11), custom_call_target="tpu_custom_call" | custom-call | flops 3623878656 | bytes 12582912 | tf_op jit(solution)/shard_map/pallas_call | solution.py:72
  41.0 5.3 %collective-permute-done.refs_1_ = f32[768,512]{1,0:T(8,128)} collective-permute-done((f32[768,512]{1,0:T(8,128)S(1)}, f32[768,512]{1,0:T(8,128)}, u32[]{:S(2)}, u32[]{:S(2)}) %collective-permute-start) | collective-permute-done | bytes 1572896 | tf_op jit(solution)/shard_map/ppermute | solution.py:137
  47.2 32.9 %collective-permute-done.3.refs_1_ = f32[768,512]{1,0:T(8,128)} collective-permute-done((f32[768,512]{1,0:T(8,128)S(1)}, f32[768,512]{1,0:T(8,128)}, u32[]{:S(2)}, u32[]{:S(2)}) %collective-permute-start.3) | collective-permute-done | bytes 1572896 | tf_op jit(solution)/shard_map/ppermute | solution.py:137
  88.6 14.8 %shard_map.71.refs_2_ = f32[1536,512]{1,0:T(8,128)} custom-call(s32[2]{0:T(128)S(1)} %pad_add_fusion.1.tab, s32[576]{0:T(1024)S(1)} %reshape.14.mask, f32[768,512]{1,0:T(8,128)} %collective-permute-done.4.refs_0_, f32[768,512]{1,0:T(8,128)} %collective-permute-done.3.refs_1_, f32[1536,6144]{1,0:T(8,128)} %refs_2_.11, f32[1536,512]{1,0:T(8,128)} %copy-done.15), custom_call_target="tpu_custom_call" | custom-call | flops 7247757312 | bytes 18874368 | tf_op jit(solution)/shard_map/pallas_call | solution.py:72
  103.4 14.9 %shard_map.70.refs_3_ = f32[1536,512]{1,0:T(8,128)} custom-call(s32[2]{0:T(128)S(1)} %pad_add_fusion.1.tab, s32[576]{0:T(1024)S(1)} %reshape.14.mask, f32[768,512]{1,0:T(8,128)} %collective-permute-done.1.refs_0_, f32[768,512]{1,0:T(8,128)} %collective-permute-done.refs_1_, f32[1536,6144]{1,0:T(8,128)} %refs_2_.11, f32[1536,512]{1,0:T(8,128)} %copy-done.14), custom_call_target="tpu_custom_call" | custom-call | flops 7247757312 | bytes 18874368 | tf_op jit(solution)/shard_map/pallas_call | solution.py:72
  120.3 30.1 %collective-permute-done.11 = f32[768,512]{1,0:T(8,128)S(1)} collective-permute-done((f32[768,512]{1,0:T(8,128)}, f32[768,512]{1,0:T(8,128)S(1)}, u32[]{:S(2)}, u32[]{:S(2)}) %collective-permute-start.11) | collective-permute-done | bytes 1572896 | tf_op jit(solution)/shard_map/ppermute | solution.py:137
  159.4 7.8 %shard_map.73.refs_3_ = f32[1536,512]{1,0:T(8,128)S(1)} custom-call(s32[1]{0:T(128)} %bitcast.9.tab, s32[576]{0:T(1024)S(1)} %reshape.14.mask, f32[768,512]{1,0:T(8,128)S(1)} %add.117.refs_0_, f32[1536,6144]{1,0:T(8,128)} %refs_2_.11, f32[1536,512]{1,0:T(8,128)} %shard_map.71.refs_2_), custom_call_target="tpu_custom_call" | custom-call | flops 3623878656 | bytes 12582912 | tf_op jit(solution)/shard_map/pallas_call | solution.py:72
  168.9 14.1 %shard_map.72.refs_3_ = f32[1536,512]{1,0:T(8,128)} custom-call(s32[2]{0:T(128)S(1)} %pad_add_fusion.2.tab, s32[576]{0:T(1024)S(1)} %reshape.14.mask, f32[768,512]{1,0:T(8,128)S(1)} %copy-done.17, f32[768,512]{1,0:T(8,128)S(1)} %add.112.refs_1_, f32[1536,6144]{1,0:T(8,128)} %refs_2_.11, f32[1536,512]{1,0:T(8,128)} %shard_map.70.refs_3_), custom_call_target="tpu_custom_call" | custom-call | flops 7247757312 | bytes 18874368 | tf_op jit(solution)/shard_map/pallas_call | solution.py:72
  183.1 7.0 %collective-permute-done.13 = f32[768,512]{1,0:T(8,128)} collective-permute-done((f32[768,512]{1,0:T(8,128)}, f32[768,512]{1,0:T(8,128)}, u32[]{:S(2)}, u32[]{:S(2)}) %collective-permute-start.13) | collective-permute-done | bytes 1572896 | tf_op jit(solution)/shard_map/ppermute | solution.py:137
  194.2 13.9 %shard_map.74.refs_2_ = f32[1536,512]{1,0:T(8,128)} custom-call(s32[2]{0:T(128)S(1)} %pad_add_fusion.3.tab, s32[576]{0:T(1024)S(1)} %reshape.14.mask, f32[768,512]{1,0:T(8,128)S(1)} %add.115.refs_0_, f32[768,512]{1,0:T(8,128)S(1)} %copy-done.20, f32[1536,6144]{1,0:T(8,128)} %refs_2_.11, f32[1536,512]{1,0:T(8,128)} %shard_map.72.refs_3_), custom_call_target="tpu_custom_call" | custom-call | flops 7247757312 | bytes 18874368 | tf_op jit(solution)/shard_map/pallas_call | solution.py:72
  208.1 15.6 %collective-permute-done.12 = f32[768,512]{1,0:T(8,128)} collective-permute-done((f32[768,512]{1,0:T(8,128)}, f32[768,512]{1,0:T(8,128)}, u32[]{:S(2)}, u32[]{:S(2)}) %collective-permute-start.12) | collective-permute-done | bytes 1572896 | tf_op jit(solution)/shard_map/ppermute | solution.py:137
  223.7 3.4 add.120.refs_0_
  227.1 8.2 %shard_map.75.acc_ref = f32[1536,512]{1,0:T(8,128)S(1)} custom-call(s32[1]{0:T(128)} %bitcast.1.tab, s32[576]{0:T(1024)S(1)} %reshape.14.mask, f32[768,512]{1,0:T(8,128)} %collective-permute-done.14.refs_0_, f32[1536,6144]{1,0:T(8,128)} %refs_2_.11, f32[1536,512]{1,0:T(8,128)} %shard_map.74.refs_2_), custom_call_target="tpu_custom_call" | custom-call | flops 3623878656 | bytes 12582912 | tf_op jit(solution)/shard_map/pallas_call | solution.py:72
  235.3 5.6 %collective-permute-start.18 = (f32[1536,512]{1,0:T(8,128)S(1)}, f32[1536,512]{1,0:T(8,128)}, u32[]{:S(2)}, u32[]{:S(2)}) collective-permute-start(f32[1536,512]{1,0:T(8,128)S(1)} %shard_map.75.acc_ref), channel_id=1, source_target_pairs={{0,8},{8,0},{1,9},{9,1},{2,10},{10,2},{3,11},{11,3},{4,12},{12,4},... | collective-permute-start | bytes 9437192 | tf_op jit(solution)/shard_map/ppermute | solution.py:230
  241.2 4.0 %collective-permute-start.16 = (f32[768,512]{1,0:T(8,128)}, f32[768,512]{1,0:T(8,128)S(1)}, u32[]{:S(2)}, u32[]{:S(2)}) collective-permute-start(f32[768,512]{1,0:T(8,128)} %collective-permute-done.4.refs_0_), channel_id=1, source_target_pairs={{2,0},{3,1},{0,2},{1,3},{6,4},{7,5},{4,6},{5,7},{10,8},{11,9},{8,1... | collective-permute-start | bytes 4718600 | tf_op jit(solution)/shard_map/ppermute | solution.py:137
  247.7 14.8 %shard_map.76.refs_3_ = f32[1536,512]{1,0:T(8,128)} custom-call(s32[2]{0:T(128)S(1)} %pad_add_fusion.3.tab, s32[576]{0:T(1024)S(1)} %reshape.14.mask, f32[768,512]{1,0:T(8,128)S(1)} %copy-done.9, f32[768,512]{1,0:T(8,128)} %collective-permute-done.15.refs_1_, f32[1536,6144]{1,0:T(8,128)} %refs_2_.11, f32[1536,512]{1,0:T(8,128)} %copy-done.13), custom_call_target="tpu_custom_call" | custom-call | flops 7247757312 | bytes 18874368 | tf_op jit(solution)/shard_map/pallas_call | solution.py:72
  262.5 2.8 add_negate_fusion.1
  265.3 4.0 %fusion.12 = f32[512,512]{1,0:T(8,128)S(1)} fusion(f32[1536,512]{1,0:T(8,128)S(1)} %add_negate_fusion.1, s32[]{:T(128)S(6)} %select_n.124, f32[768,512]{1,0:T(8,128)S(1)} %copy-done.21, f32[768,512]{1,0:T(8,128)} %collective-permute-done.14.refs_0_, f32[768,512]{1,0:T(8,128)} %collective-permute-done.1.refs_0_, f32[768,512]{1,0:T(8,128)S(1)} %copy-done.18, ...), kind=kOutput, calls=%fused_computation.19 | convolution fusion | flops 1209139200 | bytes 8912903 | tf_op jit(solution)/shard_map/dot_general | solution.py:162
  271.3 5.8 %collective-permute-done.17.refs_1_ = f32[768,512]{1,0:T(8,128)S(1)} collective-permute-done((f32[768,512]{1,0:T(8,128)}, f32[768,512]{1,0:T(8,128)S(1)}, u32[]{:S(2)}, u32[]{:S(2)}) %collective-permute-start.17) | collective-permute-done | bytes 1572896 | tf_op jit(solution)/shard_map/ppermute | solution.py:137
  277.1 2.8 collective-permute-done.16.refs_0_
  280.0 13.9 %shard_map.77.acc_ref = f32[1536,512]{1,0:T(8,128)} custom-call(s32[2]{0:T(128)S(1)} %pad_add_fusion.tab, s32[576]{0:T(1024)S(1)} %reshape.14.mask, f32[768,512]{1,0:T(8,128)S(1)} %collective-permute-done.16.refs_0_, f32[768,512]{1,0:T(8,128)S(1)} %collective-permute-done.17.refs_1_, f32[1536,6144]{1,0:T(8,128)} %refs_2_.11, f32[1536,512]{1,0:T(8,128)} %shard_map.76.refs_3_), custom_call_target="tpu_custom_call" | custom-call | flops 7247757312 | bytes 18874368 | tf_op jit(solution)/shard_map/pallas_call | solution.py:72
  295.7 4.6 %collective-permute-done.19.got_ref = f32[1536,512]{1,0:T(8,128)S(1)} collective-permute-done((f32[1536,512]{1,0:T(8,128)}, f32[1536,512]{1,0:T(8,128)S(1)}, u32[]{:S(2)}, u32[]{:S(2)}) %collective-permute-start.19) | collective-permute-done | bytes 3145760 | tf_op jit(solution)/shard_map/ppermute | solution.py:230
  300.3 2.6 add_negate_fusion
  302.9 3.4 fusion.2
  310.0 4.5 %shard_map.78.refs_0_ = f32[2,1536,512]{2,1,0:T(8,128)} custom-call(f32[1536,512]{1,0:T(8,128)S(1)} %shard_map.75.acc_ref, f32[1536,512]{1,0:T(8,128)} %collective-permute-done.18.got_ref), custom_call_target="tpu_custom_call" | custom-call | flops 1572864 | bytes 9437184 | tf_op jit(solution)/shard_map/pallas_call | solution.py:106
  325.0 54.5 %collective-permute-done.29 = f32[1024,512]{1,0:T(8,128)} collective-permute-done((f32[1024,512]{1,0:T(8,128)}, f32[1024,512]{1,0:T(8,128)}, u32[]{:S(2)}, u32[]{:S(2)}) %collective-permute-start.29) | collective-permute-done | bytes 2097184 | tf_op jit(solution)/shard_map/ppermute | solution.py:243
  379.5 3.8 select_subtract_fusion
  (133 shorter events, 61.6 us)
Async XLA Ops:
  7.0 7.0 %collective-permute-start.2 = (f32[768,512]{1,0:T(8,128)S(1)}, f32[768,512]{1,0:T(8,128)}, u32[]{:S(2)}, u32[]{:S(2)}) collective-permute-start(f32[768,512]{1,0:T(8,128)S(1)} %fusion.1.refs_0_), channel_id=1, source_target_pairs={{4,2},{5,3},{2,4},{3,5},{12,10},{13,11},{10,12},{11,13},{20,18},{2... | collective-permute-start | bytes 4718600 | tf_op jit(solution)/shard_map/ppermute | solution.py:137
  8.9 37.5 %collective-permute-start = (f32[768,512]{1,0:T(8,128)S(1)}, f32[768,512]{1,0:T(8,128)}, u32[]{:S(2)}, u32[]{:S(2)}) collective-permute-start(f32[768,512]{1,0:T(8,128)S(1)} %fusion.1.refs_0_), channel_id=1, source_target_pairs={{2,0},{3,1},{0,2},{1,3},{6,4},{7,5},{4,6},{5,7},{10,8},{11,9},{8,1... | collective-permute-start | bytes 4718600 | tf_op jit(solution)/shard_map/ppermute | solution.py:137
  12.4 34.8 %collective-permute-start.1 = (f32[768,512]{1,0:T(8,128)S(1)}, f32[768,512]{1,0:T(8,128)}, u32[]{:S(2)}, u32[]{:S(2)}) collective-permute-start(f32[768,512]{1,0:T(8,128)S(1)} %fusion.1.refs_0_), channel_id=1, source_target_pairs={{1,0},{0,1},{3,2},{2,3},{5,4},{4,5},{7,6},{6,7},{9,8},{8,9},{11,10... | collective-permute-start | bytes 4718600 | tf_op jit(solution)/shard_map/ppermute | solution.py:137
  13.6 66.4 %collective-permute-start.3 = (f32[768,512]{1,0:T(8,128)S(1)}, f32[768,512]{1,0:T(8,128)}, u32[]{:S(2)}, u32[]{:S(2)}) collective-permute-start(f32[768,512]{1,0:T(8,128)S(1)} %fusion.refs_0_), channel_id=1, source_target_pairs={{2,0},{3,1},{0,2},{1,3},{6,4},{7,5},{4,6},{5,7},{10,8},{11,9},{8,1... | collective-permute-start | bytes 4718600 | tf_op jit(solution)/shard_map/ppermute | solution.py:137
  13.7 67.2 %collective-permute-start.4 = (f32[768,512]{1,0:T(8,128)S(1)}, f32[768,512]{1,0:T(8,128)}, u32[]{:S(2)}, u32[]{:S(2)}) collective-permute-start(f32[768,512]{1,0:T(8,128)S(1)} %fusion.refs_0_), channel_id=1, source_target_pairs={{1,0},{0,1},{3,2},{2,3},{5,4},{4,5},{7,6},{6,7},{9,8},{8,9},{11,10... | collective-permute-start | bytes 4718600 | tf_op jit(solution)/shard_map/ppermute | solution.py:137
  14.0 66.9 %collective-permute-start.5 = (f32[768,512]{1,0:T(8,128)S(1)}, f32[768,512]{1,0:T(8,128)}, u32[]{:S(2)}, u32[]{:S(2)}) collective-permute-start(f32[768,512]{1,0:T(8,128)S(1)} %fusion.refs_0_), channel_id=1, source_target_pairs={{4,2},{5,3},{2,4},{3,5},{12,10},{13,11},{10,12},{11,13},{20,18},{2... | collective-permute-start | bytes 4718600 | tf_op jit(solution)/shard_map/ppermute | solution.py:137
  80.9 37.5 %collective-permute-start.7 = (f32[768,512]{1,0:T(8,128)}, f32[768,512]{1,0:T(8,128)S(1)}, u32[]{:S(2)}, u32[]{:S(2)}) collective-permute-start(f32[768,512]{1,0:T(8,128)} %collective-permute-done.2), channel_id=1, source_target_pairs={{2,0},{3,1},{4,6},{5,7},{10,8},{11,9},{12,14},{13,15},{18,16},{19,... | collective-permute-start | bytes 4718600 | tf_op jit(solution)/shard_map/ppermute | solution.py:137
  82.3 68.2 %collective-permute-start.6 = (f32[768,512]{1,0:T(8,128)}, f32[768,512]{1,0:T(8,128)S(1)}, u32[]{:S(2)}, u32[]{:S(2)}) collective-permute-start(f32[768,512]{1,0:T(8,128)} %collective-permute-done.refs_1_), channel_id=1, source_target_pairs={{1,0},{0,1},{3,2},{2,3},{5,4},{4,5},{7,6},{6,7},{9,8},{8,9},{11,10... | collective-permute-start | bytes 4718600 | tf_op jit(solution)/shard_map/ppermute | solution.py:137
  83.5 68.1 %collective-permute-start.9 = (f32[768,512]{1,0:T(8,128)}, f32[768,512]{1,0:T(8,128)}, u32[]{:S(2)}, u32[]{:S(2)}) collective-permute-start(f32[768,512]{1,0:T(8,128)} %collective-permute-done.refs_1_), channel_id=1, source_target_pairs={{4,2},{5,3},{2,4},{3,5},{12,10},{13,11},{10,12},{11,13},{20,18},{2... | collective-permute-start | bytes 4718600 | tf_op jit(solution)/shard_map/ppermute | solution.py:137
  85.3 35.0 %collective-permute-start.10 = (f32[768,512]{1,0:T(8,128)}, f32[768,512]{1,0:T(8,128)}, u32[]{:S(2)}, u32[]{:S(2)}) collective-permute-start(f32[768,512]{1,0:T(8,128)} %collective-permute-done.3.refs_1_), channel_id=1, source_target_pairs={{4,2},{5,3},{2,4},{3,5},{12,10},{13,11},{10,12},{11,13},{20,18},{2... | collective-permute-start | bytes 4718600 | tf_op jit(solution)/shard_map/ppermute | solution.py:137
  87.2 63.3 %collective-permute-start.11 = (f32[768,512]{1,0:T(8,128)}, f32[768,512]{1,0:T(8,128)S(1)}, u32[]{:S(2)}, u32[]{:S(2)}) collective-permute-start(f32[768,512]{1,0:T(8,128)} %collective-permute-done.5), channel_id=1, source_target_pairs={{2,0},{3,1},{4,6},{5,7},{10,8},{11,9},{12,14},{13,15},{18,16},{19,... | collective-permute-start | bytes 4718600 | tf_op jit(solution)/shard_map/ppermute | solution.py:137
  120.1 47.1 %copy-start.7 = (f32[768,512]{1,0:T(8,128)}, f32[768,512]{1,0:T(8,128)S(1)}, u32[]{:S(2)}) copy-start(f32[768,512]{1,0:T(8,128)S(1)} %add.112.refs_1_) | copy-start | bytes 4718596
  120.2 31.9 %collective-permute-start.8 = (f32[768,512]{1,0:T(8,128)S(1)}, f32[768,512]{1,0:T(8,128)S(1)}, u32[]{:S(2)}, u32[]{:S(2)}) collective-permute-start(f32[768,512]{1,0:T(8,128)S(1)} %add.112.refs_1_), channel_id=1, source_target_pairs={{1,0},{0,1},{3,2},{2,3},{5,4},{4,5},{7,6},{6,7},{9,8},{8,9},{11,10... | collective-permute-start | bytes 4718600 | tf_op jit(solution)/shard_map/ppermute | solution.py:137
  153.3 36.8 %collective-permute-start.13 = (f32[768,512]{1,0:T(8,128)}, f32[768,512]{1,0:T(8,128)}, u32[]{:S(2)}, u32[]{:S(2)}) collective-permute-start(f32[768,512]{1,0:T(8,128)} %collective-permute-done.9), channel_id=1, source_target_pairs={{2,0},{3,1},{4,6},{5,7},{10,8},{11,9},{12,14},{13,15},{18,16},{19,... | collective-permute-start | bytes 4718600 | tf_op jit(solution)/shard_map/ppermute | solution.py:137
  156.9 51.2 %collective-permute-start.15 = (f32[768,512]{1,0:T(8,128)S(1)}, f32[768,512]{1,0:T(8,128)}, u32[]{:S(2)}, u32[]{:S(2)}) collective-permute-start(f32[768,512]{1,0:T(8,128)S(1)} %add.117.refs_0_), channel_id=1, source_target_pairs={{1,0},{0,1},{3,2},{2,3},{5,4},{4,5},{7,6},{6,7},{9,8},{8,9},{11,10... | collective-permute-start | bytes 4718600 | tf_op jit(solution)/shard_map/ppermute | solution.py:137
  158.2 65.6 %collective-permute-start.12 = (f32[768,512]{1,0:T(8,128)}, f32[768,512]{1,0:T(8,128)}, u32[]{:S(2)}, u32[]{:S(2)}) collective-permute-start(f32[768,512]{1,0:T(8,128)} %collective-permute-done.10), channel_id=1, source_target_pairs={{2,0},{3,1},{4,6},{5,7},{10,8},{11,9},{12,14},{13,15},{18,16},{19,... | collective-permute-start | bytes 4718600 | tf_op jit(solution)/shard_map/ppermute | solution.py:137
  192.3 31.5 %collective-permute-start.14 = (f32[768,512]{1,0:T(8,128)S(1)}, f32[768,512]{1,0:T(8,128)}, u32[]{:S(2)}, u32[]{:S(2)}) collective-permute-start(f32[768,512]{1,0:T(8,128)S(1)} %add.115.refs_0_), channel_id=1, source_target_pairs={{1,0},{0,1},{3,2},{2,3},{5,4},{4,5},{7,6},{6,7},{9,8},{8,9},{11,10... | collective-permute-start | bytes 4718600 | tf_op jit(solution)/shard_map/ppermute | solution.py:137
  235.3 11.0 %collective-permute-start.18 = (f32[1536,512]{1,0:T(8,128)S(1)}, f32[1536,512]{1,0:T(8,128)}, u32[]{:S(2)}, u32[]{:S(2)}) collective-permute-start(f32[1536,512]{1,0:T(8,128)S(1)} %shard_map.75.acc_ref), channel_id=1, source_target_pairs={{0,8},{8,0},{1,9},{9,1},{2,10},{10,2},{3,11},{11,3},{4,12},{12,4},... | collective-permute-start | bytes 9437192 | tf_op jit(solution)/shard_map/ppermute | solution.py:230
  240.9 36.2 %collective-permute-start.17 = (f32[768,512]{1,0:T(8,128)}, f32[768,512]{1,0:T(8,128)S(1)}, u32[]{:S(2)}, u32[]{:S(2)}) collective-permute-start(f32[768,512]{1,0:T(8,128)} %add.120.refs_0_), channel_id=1, source_target_pairs={{1,0},{0,1},{3,2},{2,3},{5,4},{4,5},{7,6},{6,7},{9,8},{8,9},{11,10... | collective-permute-start | bytes 4718600 | tf_op jit(solution)/shard_map/ppermute | solution.py:137
  241.2 38.7 %collective-permute-start.16 = (f32[768,512]{1,0:T(8,128)}, f32[768,512]{1,0:T(8,128)S(1)}, u32[]{:S(2)}, u32[]{:S(2)}) collective-permute-start(f32[768,512]{1,0:T(8,128)} %collective-permute-done.4.refs_0_), channel_id=1, source_target_pairs={{2,0},{3,1},{0,2},{1,3},{6,4},{7,5},{4,6},{5,7},{10,8},{11,9},{8,1... | collective-permute-start | bytes 4718600 | tf_op jit(solution)/shard_map/ppermute | solution.py:137
  293.9 6.3 %collective-permute-start.19 = (f32[1536,512]{1,0:T(8,128)}, f32[1536,512]{1,0:T(8,128)S(1)}, u32[]{:S(2)}, u32[]{:S(2)}) collective-permute-start(f32[1536,512]{1,0:T(8,128)} %shard_map.77.acc_ref), channel_id=1, source_target_pairs={{0,8},{8,0},{1,9},{9,1},{2,10},{10,2},{3,11},{11,3},{4,12},{12,4},... | collective-permute-start | bytes 9437192 | tf_op jit(solution)/shard_map/ppermute | solution.py:230
  294.8 14.3 %collective-permute-start.20 = (f32[336,512]{1,0:T(8,128)S(1)}, f32[336,512]{1,0:T(8,128)S(1)}, u32[]{:S(2)}, u32[]{:S(2)}) collective-permute-start(f32[336,512]{1,0:T(8,128)S(1)} %slice.32), channel_id=1, source_target_pairs={{1,0},{0,1},{3,2},{2,3},{13,12},{12,13},{15,14},{14,15},{17,16},{1... | collective-permute-start | bytes 2064392 | tf_op jit(solution)/shard_map/ppermute | solution.py:205
  308.4 6.1 %collective-permute-start.26 = (f32[352,512]{1,0:T(8,128)S(1)}, f32[352,512]{1,0:T(8,128)S(1)}, u32[]{:S(2)}, u32[]{:S(2)}) collective-permute-start(f32[352,512]{1,0:T(8,128)S(1)} %slice.33), channel_id=1, source_target_pairs={{12,0},{13,1},{14,2},{15,3},{0,12},{1,13},{2,14},{3,15},{28,16},{2... | collective-permute-start | bytes 2162696 | tf_op jit(solution)/shard_map/ppermute | solution.py:205
  309.3 6.9 %collective-permute-start.23 = (f32[336,512]{1,0:T(8,128)S(1)}, f32[336,512]{1,0:T(8,128)S(1)}, u32[]{:S(2)}, u32[]{:S(2)}) collective-permute-start(f32[336,512]{1,0:T(8,128)S(1)} %get-tuple-element.81), channel_id=1, source_target_pairs={{2,0},{3,1},{0,2},{1,3},{14,12},{15,13},{12,14},{13,15},{18,16},{1... | collective-permute-start | bytes 2064392 | tf_op jit(solution)/shard_map/ppermute | solution.py:205
  314.6 4.6 %collective-permute-start.27 = (f32[352,512]{1,0:T(8,128)S(1)}, f32[352,512]{1,0:T(8,128)S(1)}, u32[]{:S(2)}, u32[]{:S(2)}) collective-permute-start(f32[352,512]{1,0:T(8,128)S(1)} %slice_add_fusion.1), channel_id=1, source_target_pairs={{1,0},{0,1},{3,2},{2,3},{13,12},{12,13},{15,14},{14,15},{17,16},{1... | collective-permute-start | bytes 2162696 | tf_op jit(solution)/shard_map/ppermute | solution.py:205
  315.4 4.6 %collective-permute-start.21 = (f32[336,512]{1,0:T(8,128)S(1)}, f32[336,512]{1,0:T(8,128)S(1)}, u32[]{:S(2)}, u32[]{:S(2)}) collective-permute-start(f32[336,512]{1,0:T(8,128)S(1)} %get-tuple-element.74), channel_id=1, source_target_pairs={{2,0},{3,1},{0,2},{1,3},{14,12},{15,13},{12,14},{13,15},{18,16},{1... | collective-permute-start | bytes 2064392 | tf_op jit(solution)/shard_map/ppermute | solution.py:205
  316.3 4.6 %collective-permute-start.24 = (f32[336,512]{1,0:T(8,128)S(1)}, f32[336,512]{1,0:T(8,128)S(1)}, u32[]{:S(2)}, u32[]{:S(2)}) collective-permute-start(f32[336,512]{1,0:T(8,128)S(1)} %add.131), channel_id=1, source_target_pairs={{12,0},{13,1},{14,2},{15,3},{0,12},{1,13},{2,14},{3,15},{28,16},{2... | collective-permute-start | bytes 2064392 | tf_op jit(solution)/shard_map/ppermute | solution.py:205
  319.3 2.7 collective-permute-start.28
  320.2 1.6 collective-permute-start.22
  321.0 0.9 collective-permute-start.25
  322.2 57.3 %copy-start.24 = (f32[1024,512]{1,0:T(8,128)S(1)}, f32[1024,512]{1,0:T(8,128)}, u32[]{:S(2)}) copy-start(f32[1024,512]{1,0:T(8,128)} %pad_maximum_fusion) | copy-start | bytes 6291460
  323.7 55.8 %collective-permute-start.29 = (f32[1024,512]{1,0:T(8,128)}, f32[1024,512]{1,0:T(8,128)}, u32[]{:S(2)}, u32[]{:S(2)}) collective-permute-start(f32[1024,512]{1,0:T(8,128)} %pad_maximum_fusion.1), channel_id=1, source_target_pairs={{0,8},{1,9},{2,10},{3,11},{12,4},{13,5},{14,6},{15,7},{16,24},{17,... | collective-permute-start | bytes 6291464 | tf_op jit(solution)/shard_map/ppermute | solution.py:243
  (25 other events, 131.0 us)

commit v2 on v1

--- a/solution.py
+++ b/solution.py
@@ -57,7 +57,7 @@
         out_ref[at, :] += jnp.dot(lhs, u_ref[...], preferred_element_type=jnp.float32)
 
 
-def accumulate(acc, sigma, mask, table, pieces):
+def accumulate(acc, sigma, mask, table, pieces, light=1):
     nrows, ncols = sigma.shape
     depth, width = pieces[0].shape
     n = len(pieces)
@@ -83,38 +83,90 @@
             dimension_semantics=("arbitrary",), vmem_limit_bytes=48 * 2**20
         ),
         cost_estimate=pl.CostEstimate(
-            flops=6 * n * depth * nrows * width,
-            bytes_accessed=4 * (n * depth * nrows + n * depth * width + 2 * nrows * width),
+            flops=6 * n * depth * nrows * width // light,
+            bytes_accessed=4 * n * depth * (nrows + width) // light,
             transcendentals=0,
         ),
     )(jnp.stack(table), mask, *args)
 
 
-def _negate_body(acc_ref, got_ref, *refs):
-    refs[-1][0] = -(acc_ref[...] + got_ref[...])
-
-
-def negate_into(full, acc, got, shape, s, at):
-    nrows, width = acc.shape
-    step = nrows // 3
-    tile = pl.BlockSpec((step, width), lambda i: (i, 0))
-    in_specs, args, aliases = [tile, tile], [acc, got], {}
+def _finish_body(count, place, *refs):
+    pieces, refs = refs[: 2 * count], refs[2 * count :]
+    acc_ref, got_ref = refs[:2]
+    cross_ref, term_ref, rows_ref, sem = refs[-4:]
+    t = pl.program_id(0)
+    for half in range(2):
+        for k in range(count):
+
+            @pl.when((t == 0) & (place[1] == k))
+            def _(half=half, k=k):
+                piece = pieces[half * count + k]
+                pltpu.make_async_copy(piece, rows_ref.at[half], sem.at[half]).start()
+
+        @pl.when(t == half)
+        def _(half=half):
+            pltpu.make_async_copy(pieces[0], rows_ref.at[half], sem.at[half]).wait()
+
+    halves = lambda v: (v.astype(jnp.bfloat16), v - v.astype(jnp.bfloat16).astype(jnp.float32))
+    cross = -(acc_ref[...] + got_ref[...])
+    cross_ref[0] = cross
+    c_hi, c_lo = halves(cross)
+    u_hi, u_lo = halves(rows_ref[t])
+    c_lo, u_lo = c_lo.astype(jnp.bfloat16), u_lo.astype(jnp.bfloat16)
+
+    def dot(u, v):
+        dims = (((0,), (0,)), ((), ()))
+        return lax.dot_general(u, v, dims, preferred_element_type=jnp.float32)
+
+    term = dot(u_hi, c_hi) + (dot(u_hi, c_lo) + dot(u_lo, c_hi))
+
+    @pl.when(t == 0)
+    def _():
+        term_ref[...] = term
+
+    @pl.when(t > 0)
+    def _():
+        term_ref[...] += term
+
+
+def finish(full, acc, got, place, near, far, shape, s):
+    depth, width = near[0].shape
+    anywhere = pl.BlockSpec(memory_space=pl.ANY)
+    tile = pl.BlockSpec((depth, width), lambda t, place: ((t + place[0]) % 2, 0))
+    args = [*near, *far, acc, got]
+    in_specs = [anywhere] * (len(near) + len(far)) + [tile, tile]
+    aliases = {}
     if full is not None:
-        in_specs.append(pl.BlockSpec(memory_space=pl.ANY))
+        aliases = {len(args) + 1: 0}
         args.append(full)
-        aliases = {2: 0}
+        in_specs.append(anywhere)
     return pl.pallas_call(
-        _negate_body,
-        grid=(3,),
-        in_specs=in_specs,
-        out_specs=pl.BlockSpec((1, step, width), lambda i: (s, i, at // width)),
-        out_shape=jax.ShapeDtypeStruct(shape, jnp.float32),
+        functools.partial(_finish_body, len(near)),
+        grid_spec=pltpu.PrefetchScalarGridSpec(
+            num_scalar_prefetch=1,
+            grid=(2,),
+            in_specs=in_specs,
+            out_specs=[
+                pl.BlockSpec((1, depth, width), lambda t, place: (s, (t + place[0]) % 2, 0)),
+                pl.BlockSpec((width, width), lambda t, place: (0, 0)),
+            ],
+            scratch_shapes=[
+                pltpu.VMEM((2, depth, width), jnp.float32),
+                pltpu.SemaphoreType.DMA((2,)),
+            ],
+        ),
+        out_shape=[
+            jax.ShapeDtypeStruct(shape, jnp.float32),
+            jax.ShapeDtypeStruct((width, width), jnp.float32),
+        ],
         input_output_aliases=aliases,
-        compiler_params=pltpu.CompilerParams(vmem_limit_bytes=32 * 2**20),
+        compiler_params=pltpu.CompilerParams(
+            dimension_semantics=("arbitrary",), vmem_limit_bytes=40 * 2**20
+        ),
         cost_estimate=pl.CostEstimate(
-            flops=2 * nrows * width, bytes_accessed=12 * nrows * width, transcendentals=0
-        ),
-    )(*args)
+            flops=depth * width, bytes_accessed=depth * width, transcendentals=0
+        ),
+    )(place, *args)
 
 
 def after(value, *deps):
@@ -138,7 +190,7 @@
 
     ox = lambda i: i ^ 1
     za = lambda i: i ^ 2
-    zb = lambda i: i ^ 4
+    outer = lambda i: i - 2 if i < ncol // 2 else i + 2
 
     row_mask = jnp.repeat(row_pattern.astype(jnp.float32), BLK, axis=1)
     local = lax.dynamic_slice_in_dim(row_mask, (r * ncol + c) * own_rows, own_rows, 1)
@@ -154,22 +206,23 @@
     near = [2 * p + x for p in planes]
     far = [2 * p + 1 - x for p in planes]
 
-    def add(acc, *terms):
-        return accumulate(acc, sigma_anc, mask, [i for i, _ in terms], [p for _, p in terms])
+    def add(acc, *terms, light=1):
+        tables, pieces = [i for i, _ in terms], [p for _, p in terms]
+        return accumulate(acc, sigma_anc, mask, tables, pieces, light)
 
     def tdot(a, b, precision):
         dims = (((0,), (0,)), ((), ()))
         return lax.dot_general(a, b, dims, precision=precision)
 
     a0, b0 = lax.optimization_barrier((scale(0, 0, width), scale(1, 0, width)))
-    a1, ax0, am = recv(za, a0), recv(ox, a0), recv(inner, a0, mids)
+    ax0, a1, am = recv(ox, a0), recv(za, a0), recv(inner, a0, mids)
     b1, bx0 = recv(za, b0), recv(ox, b0)
     acc_a = add(None, (near[0], a0))
     acc_b = add(None, (near[0], b0))
     bm = recv(inner, after(b0, am), mids)
-    square = jnp.concatenate([tdot(d, d, HIGHEST) for d in (diag_inverse[0], diag_inverse[1])])
-    a1, ax0, am, b1, bx0, bm, acc_a, acc_b, square = lax.optimization_barrier(
-        (a1, ax0, am, b1, bx0, bm, acc_a, acc_b, square)
+    square = jnp.stack([tdot(diag_inverse[i], diag_inverse[i], HIGHEST) for i in range(ns)])
+    a1, ax0, am, acc_a, acc_b, square = lax.optimization_barrier(
+        (a1, ax0, am, acc_a, acc_b, square)
     )
     ae, an, ax1 = recv(inner, am, ends), recv(inner, a1, mids), recv(ox, a1)
     be, bn = recv(inner, bm, ends), recv(inner, b1, mids)
@@ -177,71 +230,54 @@
     acc_b = add(acc_b, (far[0], bx0), (near[1], b1))
     a2 = am + ae
     ax2 = recv(ox, after(a2, acc_a, acc_b))
-    ax1, ax2, an, bn, a2, be, acc_a, acc_b = lax.optimization_barrier(
-        (ax1, ax2, an, bn, a2, be, acc_a, acc_b)
+    ax1, an, bn, a2, bm, be, acc_a, acc_b = lax.optimization_barrier(
+        (ax1, an, bn, a2, bm, be, acc_a, acc_b)
     )
     b2 = bm + be
     af, bf, bx2 = recv(inner, an, ends), recv(inner, bn, ends), recv(ox, b2)
-    acc_a = add(acc_a, (far[1], ax1), (near[2], a2))
-    acc_b = add(acc_b, (near[2], b2))
+    acc_b = add(acc_b, (near[2], after(b2, ax2)))
+    acc_a = add(acc_a, (far[1], after(ax1, ax2)), (near[2], a2))
     a3 = an + af
     ax3 = recv(ox, after(a3, acc_a, acc_b))
     acc_a = add(acc_a, (near[3], a3), (far[2], ax2))
-    bf, bn, ax3, bx2, bx0, acc_a, acc_b = lax.optimization_barrier(
-        (bf, bn, ax3, bx2, bx0, acc_a, acc_b)
-    )
+    bf, bn, bx0, acc_a, acc_b = lax.optimization_barrier((bf, bn, bx0, acc_a, acc_b))
     b3 = bn + bf
     bx1, bx3 = recv(za, bx0), recv(ox, b3)
-    acc_a = add(acc_a, (far[3], after(ax3, b3)))
+    acc_b = add(acc_b, (near[3], b3), (far[2], bx2), light=1000)
+    acc_a = add(acc_a, (far[3], after(ax3, acc_b)), light=1000)
 
     own_r = lambda i: i // (ncol // 2)
     holder = lambda i: own_r(i) * ncol + i
     other = lambda i: (1 - own_r(i)) * ncol + i
     is_holder = r == c // (ncol // 2)
+    def recv_holder(frm, v, who=every):
+        pairs = [(holder(src), holder(dst)) for src, dst in mesh_pairs(frm, who)]
+        return lax.ppermute(v, ("row", "col"), pairs)
+
+    def total(term):
+        size = term.shape[0] // 2
+        low, high = term[:size], term[size:]
+        v = jnp.where(x == 0, low, high) + recv_holder(ox, jnp.where(x == 0, high, low))
+        v = v + recv_holder(outer, v, mids)
+        v = v + recv_holder(inner, v, mids)
+        v = jnp.where((z == 0) | (z == 3), recv_holder(inner, v, ends), v)
+        w = recv_holder(ox, v)
+        term = jnp.where(x == 0, jnp.concatenate([v, w]), jnp.concatenate([w, v]))
+        pairs = [(holder(i), other(i)) for i in range(ncol)]
+        return jnp.where(is_holder, term, lax.ppermute(term, ("row", "col"), pairs))
+
     wanted = c % (ncol // 2)
-
-    def recv_holder(frm, v):
-        pairs = [(holder(frm(i)), holder(i)) for i in range(ncol)]
-        return lax.ppermute(v, ("row", "col"), pairs)
-
-    def choose(p0, p1, p2, p3):
-        first = jnp.where(wanted == planes[0], p0, p1)
-        second = jnp.where(wanted == planes[2], p2, p3)
-        return jnp.where((wanted == planes[0]) | (wanted == planes[1]), first, second)
-
-    def total(term, parts, work):
-        size = term.shape[0] // parts // 8 * 8
-        cuts = [i * size for i in range(parts)] + [term.shape[0]]
-        ways = [ox, za, zb]
-        values = [term[cuts[k] : cuts[k + 1]] for k in range(parts)]
-        for step in range(3):
-            values = [v + recv_holder(ways[(k + step) % 3], v) for k, v in enumerate(values)]
-            if step < len(work):
-                values = [after(v, work[step]) for v in values]
-        return jnp.concatenate(values)
-
-    def local_term(acc, got, same, cros):
-        same, cros = choose(*same), choose(*cros)
-        cross = -(acc + got)
-        out_same = lax.dynamic_slice_in_dim(cross, x * own_rows, own_rows, 0)
-        out_cros = lax.dynamic_slice_in_dim(cross, (1 - x) * own_rows, own_rows, 0)
-        return tdot(same, out_same, HIGH) + tdot(cros, out_cros, HIGH)
-
+    pick = sum(k * (wanted == p).astype(jnp.int32) for k, p in enumerate(planes))
+    place = jnp.stack([x, pick])
     swap = lambda v: lax.ppermute(v, "row", [(0, 1), (1, 0)])
     shape = (ns, grid_rows, width)
     got_a = swap(acc_a)
-    acc_b = add(acc_b, (near[3], after(b3, got_a)), (far[2], bx2))
+    acc_b = add(acc_b, (far[1], bx1), (far[3], bx3))
+    got_b = swap(acc_b)
     got_a = after(got_a, acc_b)
-    term_a = local_term(acc_a, got_a, (a0, a1, a2, a3), (ax0, ax1, ax2, ax3))
-    acc_b = add(acc_b, (far[1], bx1), (far[3], after(bx3, term_a)))
-    got_b = swap(acc_b)
-    term_b = local_term(acc_b, got_b, (b0, b1, b2, b3), (bx0, bx1, bx2, bx3))
-    half = negate_into(None, acc_a, got_a, shape, 0, 0)
-    full = negate_into(half, acc_b, got_b, shape, 1, 0)
-    term = total(jnp.concatenate([term_a, term_b]), 3, (half, full))
-    pairs = [(holder(i), other(i)) for i in range(ncol)]
-    term = jnp.where(is_holder, term, lax.ppermute(term, ("row", "col"), pairs))
-    return full, (square - term).reshape(diag_inverse.shape)
+    full, term_a = finish(None, acc_a, got_a, place, (a0, a1, a2, a3), (ax0, ax1, ax2, ax3), shape, 0)
+    full, term_b = finish(full, acc_b, got_b, place, (b0, b1, b2, b3), (bx0, bx1, bx2, bx3), shape, 1)
+    return full, square - jnp.stack([total(term_a), total(term_b)])
 
 
 def plain_path(sigma_anc, factor_rows, diag_inverse, row_pattern, anc_pattern):

time: 387 us -> 368 us (0.951)
  waiting for transfers between devices: 162 us -> 145 us
  matrix products: 19.6 us -> 8.29 us
  Pallas kernels: 123 us -> 134 us
    dot_general x6 -> x2, matrix products: 16.6 us -> 5.39 us  [tdot(): return lax.dot_general(a, b, dims, precision=precision)]
    ppermute x18, waiting for transfers between devices: 102 us -> 92.2 us  [recv(): return lax.ppermute(v, 'col', mesh_pairs(frm, who))]
    pallas_call x2, Pallas kernels: 6.65 us -> 13.8 us  [finish(): pl.pallas_call(functools.partial(_finish_body, len(near)), grid_spec=pltp...]
    ppermute x2, waiting for transfers between devices: 5.59 us -> 0.01 us  [grid_path(): swap = lambda v: lax.ppermute(v, 'row', [(0, 1), (1, 0)])]
    neg x2 -> x0, other arithmetic: 5.46 us -> none  [local_term(): cross = -(acc + got)]
    pallas_call x10, Pallas kernels: 116 us -> 121 us  [accumulate(): pl.pallas_call(functools.partial(_accumulate_body, n, row_step, ncols //...]
    another operation x0 -> x4, other arithmetic: none -> 4.44 us  [the longest x2 2.87 us: grid_path(): return (full, square - jnp.stack([total(term_a), total(term_b)]))]
    unnamed x56 -> x20, local copies, waits for them, and re-layouts: 10.8 us -> 7.94 us
  transfers between devices with their start and end apart: 30 -> 32, of which waited for: 13 -> 10; matrix products, arithmetic and copies ran while one was open for 8% -> 7% of each run, Pallas kernels for 26% -> 37%
where the time goes in v2:
time: 368 us; the launch traced here: 362 us
  waiting for transfers between devices  145 us (39%)
  Pallas kernels  134 us (36%)
  starting transfers between devices  39.8 us (11%)
  other arithmetic  23.8 us (6%)
  local copies, waits for them, and re-layouts  8.8 us (2%)
  matrix products  8.29 us (2%)
    pallas_call x10, Pallas kernels, accumulate(): pl.pallas_call(functools.partial(_accumulate_body, n, row_step, ncols //...  121 us
    ppermute x18, waiting for transfers between devices, recv(): return lax.ppermute(v, 'col', mesh_pairs(frm, who))  92.2 us
    ppermute x2, waiting for transfers between devices, total(): return jnp.where(is_holder, term, lax.ppermute(term, ('row', 'col'), pairs))  52.7 us
    ppermute x18, starting transfers between devices, recv(): return lax.ppermute(v, 'col', mesh_pairs(frm, who))  22.4 us
    pallas_call x2, Pallas kernels, finish(): pl.pallas_call(functools.partial(_finish_body, len(near)), grid_spec=pltp...  13.8 us
    unnamed x20, local copies, waits for them, and re-layouts  7.94 us
    ppermute x2, starting transfers between devices, grid_path(): swap = lambda v: lax.ppermute(v, 'row', [(0, 1), (1, 0)])  7.87 us
  transfers between devices with their start and end apart: 32, of which 10 were waited for; matrix products, arithmetic and copies ran while one was open for 7% of the time, Pallas kernels for 37%

profile of v2, /device:TPU:1, one launch (start us, length us, event | category | flops | bytes accessed | tf_op | source)
XLA Modules:
  0.0 361.6 jit_solution(5087053478177916482)
XLA Ops:
  1.5 2.3 broadcast_multiply_fusion
  8.8 3.6 collective-permute-start.1
  14.8 3.5 convolution_bitcast_fusion
  18.3 1.9 convolution_bitcast_fusion.1
  21.7 2.4 collective-permute-start.8
  24.1 6.7 %shard_map.68.refs_3_ = f32[1536,512]{1,0:T(8,128)S(1)} custom-call(s32[1]{0:T(128)} %bitcast.6.tab, s32[576]{0:T(1024)S(1)} %reshape.12.mask, f32[768,512]{1,0:T(8,128)S(1)} %fusion.1.refs_0_, f32[1536,6144]{1,0:T(8,128)} %refs_1_.7), custom_call_target="tpu_custom_call" | custom-call | flops 3623878656 | bytes 6291456 | tf_op jit(solution)/shard_map/pallas_call | solution.py:72
  32.5 6.7 %shard_map.69.refs_3_ = f32[1536,512]{1,0:T(8,128)S(1)} custom-call(s32[1]{0:T(128)} %bitcast.6.tab, s32[576]{0:T(1024)S(1)} %reshape.12.mask, f32[768,512]{1,0:T(8,128)S(1)} %fusion.refs_0_, f32[1536,6144]{1,0:T(8,128)} %refs_1_.7), custom_call_target="tpu_custom_call" | custom-call | flops 3623878656 | bytes 6291456 | tf_op jit(solution)/shard_map/pallas_call | solution.py:72
  40.9 5.4 %collective-permute-done.1.refs_1_ = f32[768,512]{1,0:T(8,128)} collective-permute-done((f32[768,512]{1,0:T(8,128)S(1)}, f32[768,512]{1,0:T(8,128)}, u32[]{:S(2)}, u32[]{:S(2)}) %collective-permute-start.1) | collective-permute-done | bytes 1572896 | tf_op jit(solution)/shard_map/ppermute | solution.py:189
  49.7 14.8 %shard_map.70.refs_3_ = f32[1536,512]{1,0:T(8,128)} custom-call(s32[2]{0:T(128)S(1)} %pad_add_fusion.1.tab, s32[576]{0:T(1024)S(1)} %reshape.12.mask, f32[768,512]{1,0:T(8,128)} %collective-permute-done.2.refs_0_.refs_4_, f32[768,512]{1,0:T(8,128)} %collective-permute-done.1.refs_1_, f32[1536,6144]{1,0:T(8,128)} %refs_1_.7, f32[1536,512]{1,0:T(8,128)} %copy-done.2), custom_call_target="tpu_custom_call" | custom-call | flops 7247757312 | bytes 12582912 | tf_op jit(solution)/shard_map/pallas_call | solution.py:72
  64.5 15.5 %collective-permute-done.refs_1_ = f32[768,512]{1,0:T(8,128)} collective-permute-done((f32[768,512]{1,0:T(8,128)S(1)}, f32[768,512]{1,0:T(8,128)}, u32[]{:S(2)}, u32[]{:S(2)}) %collective-permute-start) | collective-permute-done | bytes 1572896 | tf_op jit(solution)/shard_map/ppermute | solution.py:189
  85.1 14.9 %shard_map.71.refs_2_ = f32[1536,512]{1,0:T(8,128)} custom-call(s32[2]{0:T(128)S(1)} %pad_add_fusion.1.tab, s32[576]{0:T(1024)S(1)} %reshape.12.mask, f32[768,512]{1,0:T(8,128)} %collective-permute-done.10.refs_0_.refs_4_, f32[768,512]{1,0:T(8,128)} %collective-permute-done.refs_1_, f32[1536,6144]{1,0:T(8,128)} %refs_1_.7, f32[1536,512]{1,0:T(8,128)} %copy-done), custom_call_target="tpu_custom_call" | custom-call | flops 7247757312 | bytes 12582912 | tf_op jit(solution)/shard_map/pallas_call | solution.py:72
  100.0 13.7 %collective-permute-done.7 = f32[768,512]{1,0:T(8,128)} collective-permute-done((f32[768,512]{1,0:T(8,128)}, f32[768,512]{1,0:T(8,128)}, u32[]{:S(2)}, u32[]{:S(2)}) %collective-permute-start.7) | collective-permute-done | bytes 1572896 | tf_op jit(solution)/shard_map/ppermute | solution.py:189
  113.7 3.4 add.90.refs_1_.refs_2_
  119.4 27.9 %collective-permute-done.9 = f32[768,512]{1,0:T(8,128)} collective-permute-done((f32[768,512]{1,0:T(8,128)}, f32[768,512]{1,0:T(8,128)}, u32[]{:S(2)}, u32[]{:S(2)}) %collective-permute-start.9) | collective-permute-done | bytes 1572896 | tf_op jit(solution)/shard_map/ppermute | solution.py:189
  148.9 3.4 add.93.refs_0_.refs_2_
  154.8 8.2 %shard_map.74.refs_3_ = f32[1536,512]{1,0:T(8,128)S(1)} custom-call(s32[1]{0:T(128)} %bitcast.14.tab, s32[576]{0:T(1024)S(1)} %reshape.12.mask, f32[768,512]{1,0:T(8,128)} %add.93.refs_0_.refs_2_, f32[1536,6144]{1,0:T(8,128)} %refs_1_.7, f32[1536,512]{1,0:T(8,128)} %shard_map.71.refs_2_), custom_call_target="tpu_custom_call" | custom-call | flops 3623878656 | bytes 6291456 | tf_op jit(solution)/shard_map/pallas_call | solution.py:72
  164.7 14.6 %shard_map.72.refs_3_ = f32[1536,512]{1,0:T(8,128)} custom-call(s32[2]{0:T(128)S(1)} %pad_add_fusion.3.tab, s32[576]{0:T(1024)S(1)} %reshape.12.mask, f32[768,512]{1,0:T(8,128)S(1)} %copy-done.4, f32[768,512]{1,0:T(8,128)} %add.90.refs_1_.refs_2_, f32[1536,6144]{1,0:T(8,128)} %refs_1_.7, f32[1536,512]{1,0:T(8,128)} %shard_map.70.refs_3_), custom_call_target="tpu_custom_call" | custom-call | flops 7247757312 | bytes 12582912 | tf_op jit(solution)/shard_map/pallas_call | solution.py:72
  179.3 9.1 %collective-permute-done.12 = f32[768,512]{1,0:T(8,128)} collective-permute-done((f32[768,512]{1,0:T(8,128)}, f32[768,512]{1,0:T(8,128)}, u32[]{:S(2)}, u32[]{:S(2)}) %collective-permute-start.12) | collective-permute-done | bytes 1572896 | tf_op jit(solution)/shard_map/ppermute | solution.py:189
  188.4 3.4 add.96.refs_0_.refs_3_
  191.9 14.8 %shard_map.73.refs_2_ = f32[1536,512]{1,0:T(8,128)} custom-call(s32[2]{0:T(128)S(1)} %pad_add_fusion.2.tab, s32[576]{0:T(1024)S(1)} %reshape.12.mask, f32[768,512]{1,0:T(8,128)} %add.96.refs_0_.refs_3_, f32[768,512]{1,0:T(8,128)} %collective-permute-done.13.refs_1_.refs_6_, f32[1536,6144]{1,0:T(8,128)} %refs_1_.7, f32[1536,512]{1,0:T(8,128)} %shard_map.72.refs_3_), custom_call_target="tpu_custom_call" | custom-call | flops 7247757312 | bytes 12582912 | tf_op jit(solution)/shard_map/pallas_call | solution.py:72
  206.7 15.3 %collective-permute-done.11 = f32[768,512]{1,0:T(8,128)S(1)} collective-permute-done((f32[768,512]{1,0:T(8,128)}, f32[768,512]{1,0:T(8,128)S(1)}, u32[]{:S(2)}, u32[]{:S(2)}) %collective-permute-start.11) | collective-permute-done | bytes 1572896 | tf_op jit(solution)/shard_map/ppermute | solution.py:189
  222.1 2.9 add.99.refs_0_.refs_3_
  225.3 15.2 %shard_map.75.refs_3_ = f32[1536,512]{1,0:T(8,128)} custom-call(s32[2]{0:T(128)S(1)} %pad_add_fusion.2.tab, s32[576]{0:T(1024)S(1)} %reshape.12.mask, f32[768,512]{1,0:T(8,128)} %add.99.refs_0_.refs_3_, f32[768,512]{1,0:T(8,128)} %collective-permute-done.15.refs_1_.refs_6_, f32[1536,6144]{1,0:T(8,128)} %refs_1_.7, f32[1536,512]{1,0:T(8,128)} %copy-done.1), custom_call_target="tpu_custom_call" | custom-call | flops 7247757 | bytes 12582 | tf_op jit(solution)/shard_map/pallas_call | solution.py:72
  240.4 9.9 %shard_map.77.refs_8_ = f32[1536,512]{1,0:T(8,128)} custom-call(s32[1]{0:T(128)} %bitcast.15.tab, s32[576]{0:T(1024)S(1)} %reshape.12.mask, f32[768,512]{1,0:T(8,128)} %collective-permute-done.18.refs_0_.refs_7_, f32[1536,6144]{1,0:T(8,128)} %refs_1_.7, f32[1536,512]{1,0:T(8,128)} %shard_map.73.refs_2_), custom_call_target="tpu_custom_call" | custom-call | flops 3623878 | bytes 6291 | tf_op jit(solution)/shard_map/pallas_call | solution.py:72
  250.3 3.9 %collective-permute-start.19 = (f32[1536,512]{1,0:T(8,128)}, f32[1536,512]{1,0:T(8,128)}, u32[]{:S(2)}, u32[]{:S(2)}) collective-permute-start(f32[1536,512]{1,0:T(8,128)} %shard_map.77.refs_8_), channel_id=1, source_target_pairs={{0,8},{8,0},{1,9},{9,1},{2,10},{10,2},{3,11},{11,3},{4,12},{12,4},... | collective-permute-start | bytes 9437192 | tf_op jit(solution)/shard_map/ppermute | solution.py:272
  254.2 4.4 %collective-permute-done.16.refs_1_.refs_7_ = f32[768,512]{1,0:T(8,128)} collective-permute-done((f32[768,512]{1,0:T(8,128)}, f32[768,512]{1,0:T(8,128)}, u32[]{:S(2)}, u32[]{:S(2)}) %collective-permute-start.16) | collective-permute-done | bytes 1572896 | tf_op jit(solution)/shard_map/ppermute | solution.py:189
  258.6 14.8 %shard_map.76.refs_8_ = f32[1536,512]{1,0:T(8,128)} custom-call(s32[2]{0:T(128)S(1)} %pad_add_fusion.4.tab, s32[576]{0:T(1024)S(1)} %reshape.12.mask, f32[768,512]{1,0:T(8,128)} %collective-permute-done.14.refs_0_.refs_5_, f32[768,512]{1,0:T(8,128)} %collective-permute-done.16.refs_1_.refs_7_, f32[1536,6144]{1,0:T(8,128)} %refs_1_.7, ...), custom_call_target="tpu_custom_call" | custom-call | flops 7247757312 | bytes 12582912 | tf_op jit(solution)/shard_map/pallas_call | solution.py:72
  273.4 4.0 %collective-permute-start.17 = (f32[1536,512]{1,0:T(8,128)}, f32[1536,512]{1,0:T(8,128)}, u32[]{:S(2)}, u32[]{:S(2)}) collective-permute-start(f32[1536,512]{1,0:T(8,128)} %shard_map.76.refs_8_), channel_id=1, source_target_pairs={{0,8},{8,0},{1,9},{9,1},{2,10},{10,2},{3,11},{11,3},{4,12},{12,4},... | collective-permute-start | bytes 9437192 | tf_op jit(solution)/shard_map/ppermute | solution.py:272
  278.9 6.9 %shard_map.78 = (f32[2,1536,512]{2,1,0:T(8,128)}, f32[512,512]{1,0:T(8,128)S(1)}) custom-call(s32[2]{0:T(128)S(1)} %pad_add_fusion.place, f32[768,512]{1,0:T(8,128)S(1)} %fusion.1.refs_0_, f32[768,512]{1,0:T(8,128)} %collective-permute-done.1.refs_1_, f32[768,512]{1,0:T(8,128)} %add.90.refs_1_.refs_2_, f32[768,512]{1,0:T(8,128)} %add.96.refs_0_.refs_3_, ...), custom_call_target="tpu_custom_call" | custom-call | flops 393216 | bytes 393216 | tf_op jit(solution)/shard_map/pallas_call | solution.py:143
  286.6 6.9 %shard_map.79 = (f32[2,1536,512]{2,1,0:T(8,128)}, f32[512,512]{1,0:T(8,128)S(1)}) custom-call(s32[2]{0:T(128)S(1)} %pad_add_fusion.place, f32[768,512]{1,0:T(8,128)S(1)} %fusion.refs_0_, f32[768,512]{1,0:T(8,128)} %collective-permute-done.refs_1_, f32[768,512]{1,0:T(8,128)} %add.93.refs_0_.refs_2_, ...), custom_call_target="tpu_custom_call", output_to_operand_aliasing={{0}: (11, {})} | custom-call | flops 393216 | bytes 393216 | tf_op jit(solution)/shard_map/pallas_call | solution.py:143
  303.8 46.5 %collective-permute-done.25 = f32[512,512]{1,0:T(8,128)} collective-permute-done((f32[512,512]{1,0:T(8,128)S(1)}, f32[512,512]{1,0:T(8,128)}, u32[]{:S(2)}, u32[]{:S(2)}) %collective-permute-start.25) | collective-permute-done | bytes 1048608 | tf_op jit(solution)/shard_map/ppermute | solution.py:267
  351.8 6.2 %collective-permute-done.31 = f32[512,512]{1,0:T(8,128)} collective-permute-done((f32[512,512]{1,0:T(8,128)S(1)}, f32[512,512]{1,0:T(8,128)}, u32[]{:S(2)}, u32[]{:S(2)}) %collective-permute-start.31) | collective-permute-done | bytes 1048608 | tf_op jit(solution)/shard_map/ppermute | solution.py:267
  (98 shorter events, 47.0 us)
Async XLA Ops:
  7.0 14.7 %collective-permute-start.3 = (f32[768,512]{1,0:T(8,128)S(1)}, f32[768,512]{1,0:T(8,128)}, u32[]{:S(2)}, u32[]{:S(2)}) collective-permute-start(f32[768,512]{1,0:T(8,128)S(1)} %fusion.1.refs_0_), channel_id=1, source_target_pairs={{4,2},{5,3},{2,4},{3,5},{12,10},{13,11},{10,12},{11,13},{20,18},{2... | collective-permute-start | bytes 4718600 | tf_op jit(solution)/shard_map/ppermute | solution.py:189
  8.8 37.5 %collective-permute-start.1 = (f32[768,512]{1,0:T(8,128)S(1)}, f32[768,512]{1,0:T(8,128)}, u32[]{:S(2)}, u32[]{:S(2)}) collective-permute-start(f32[768,512]{1,0:T(8,128)S(1)} %fusion.1.refs_0_), channel_id=1, source_target_pairs={{2,0},{3,1},{0,2},{1,3},{6,4},{7,5},{4,6},{5,7},{10,8},{11,9},{8,1... | collective-permute-start | bytes 4718600 | tf_op jit(solution)/shard_map/ppermute | solution.py:189
  12.4 34.7 %collective-permute-start.2 = (f32[768,512]{1,0:T(8,128)S(1)}, f32[768,512]{1,0:T(8,128)}, u32[]{:S(2)}, u32[]{:S(2)}) collective-permute-start(f32[768,512]{1,0:T(8,128)S(1)} %fusion.1.refs_0_), channel_id=1, source_target_pairs={{1,0},{0,1},{3,2},{2,3},{5,4},{4,5},{7,6},{6,7},{9,8},{8,9},{11,10... | collective-permute-start | bytes 4718600 | tf_op jit(solution)/shard_map/ppermute | solution.py:189
  13.6 66.4 %collective-permute-start = (f32[768,512]{1,0:T(8,128)S(1)}, f32[768,512]{1,0:T(8,128)}, u32[]{:S(2)}, u32[]{:S(2)}) collective-permute-start(f32[768,512]{1,0:T(8,128)S(1)} %fusion.refs_0_), channel_id=1, source_target_pairs={{2,0},{3,1},{0,2},{1,3},{6,4},{7,5},{4,6},{5,7},{10,8},{11,9},{8,1... | collective-permute-start | bytes 4718600 | tf_op jit(solution)/shard_map/ppermute | solution.py:189
  13.7 68.2 %collective-permute-start.10 = (f32[768,512]{1,0:T(8,128)S(1)}, f32[768,512]{1,0:T(8,128)}, u32[]{:S(2)}, u32[]{:S(2)}) collective-permute-start(f32[768,512]{1,0:T(8,128)S(1)} %fusion.refs_0_), channel_id=1, source_target_pairs={{1,0},{0,1},{3,2},{2,3},{5,4},{4,5},{7,6},{6,7},{9,8},{8,9},{11,10... | collective-permute-start | bytes 4718600 | tf_op jit(solution)/shard_map/ppermute | solution.py:189
  21.7 62.0 %collective-permute-start.8 = (f32[768,512]{1,0:T(8,128)S(1)}, f32[768,512]{1,0:T(8,128)}, u32[]{:S(2)}, u32[]{:S(2)}) collective-permute-start(f32[768,512]{1,0:T(8,128)S(1)} %fusion.refs_0_), channel_id=1, source_target_pairs={{4,2},{5,3},{2,4},{3,5},{12,10},{13,11},{10,12},{11,13},{20,18},{2... | collective-permute-start | bytes 4718600 | tf_op jit(solution)/shard_map/ppermute | solution.py:189
  47.1 66.6 %collective-permute-start.7 = (f32[768,512]{1,0:T(8,128)}, f32[768,512]{1,0:T(8,128)}, u32[]{:S(2)}, u32[]{:S(2)}) collective-permute-start(f32[768,512]{1,0:T(8,128)} %collective-permute-done.3), channel_id=1, source_target_pairs={{2,0},{3,1},{4,6},{5,7},{10,8},{11,9},{12,14},{13,15},{18,16},{19,... | collective-permute-start | bytes 4718600 | tf_op jit(solution)/shard_map/ppermute | solution.py:189
  48.5 69.8 %collective-permute-start.4 = (f32[768,512]{1,0:T(8,128)}, f32[768,512]{1,0:T(8,128)S(1)}, u32[]{:S(2)}, u32[]{:S(2)}) collective-permute-start(f32[768,512]{1,0:T(8,128)} %collective-permute-done.1.refs_1_), channel_id=1, source_target_pairs={{1,0},{0,1},{3,2},{2,3},{5,4},{4,5},{7,6},{6,7},{9,8},{8,9},{11,10... | collective-permute-start | bytes 4718600 | tf_op jit(solution)/shard_map/ppermute | solution.py:189
  80.0 39.5 %collective-permute-start.5 = (f32[768,512]{1,0:T(8,128)}, f32[768,512]{1,0:T(8,128)}, u32[]{:S(2)}, u32[]{:S(2)}) collective-permute-start(f32[768,512]{1,0:T(8,128)} %collective-permute-done.1.refs_1_), channel_id=1, source_target_pairs={{4,2},{5,3},{2,4},{3,5},{12,10},{13,11},{10,12},{11,13},{20,18},{2... | collective-permute-start | bytes 4718600 | tf_op jit(solution)/shard_map/ppermute | solution.py:189
  81.8 37.6 %collective-permute-start.6 = (f32[768,512]{1,0:T(8,128)}, f32[768,512]{1,0:T(8,128)}, u32[]{:S(2)}, u32[]{:S(2)}) collective-permute-start(f32[768,512]{1,0:T(8,128)} %collective-permute-done.refs_1_), channel_id=1, source_target_pairs={{4,2},{5,3},{2,4},{3,5},{12,10},{13,11},{10,12},{11,13},{20,18},{2... | collective-permute-start | bytes 4718600 | tf_op jit(solution)/shard_map/ppermute | solution.py:189
  83.7 63.7 %collective-permute-start.9 = (f32[768,512]{1,0:T(8,128)}, f32[768,512]{1,0:T(8,128)}, u32[]{:S(2)}, u32[]{:S(2)}) collective-permute-start(f32[768,512]{1,0:T(8,128)} %collective-permute-done.8), channel_id=1, source_target_pairs={{2,0},{3,1},{4,6},{5,7},{10,8},{11,9},{12,14},{13,15},{18,16},{19,... | collective-permute-start | bytes 4718600 | tf_op jit(solution)/shard_map/ppermute | solution.py:189
  117.1 36.4 %collective-permute-start.13 = (f32[768,512]{1,0:T(8,128)}, f32[768,512]{1,0:T(8,128)}, u32[]{:S(2)}, u32[]{:S(2)}) collective-permute-start(f32[768,512]{1,0:T(8,128)} %add.90.refs_1_.refs_2_), channel_id=1, source_target_pairs={{1,0},{0,1},{3,2},{2,3},{5,4},{4,5},{7,6},{6,7},{9,8},{8,9},{11,10... | collective-permute-start | bytes 4718600 | tf_op jit(solution)/shard_map/ppermute | solution.py:189
  147.4 41.0 %collective-permute-start.12 = (f32[768,512]{1,0:T(8,128)}, f32[768,512]{1,0:T(8,128)}, u32[]{:S(2)}, u32[]{:S(2)}) collective-permute-start(f32[768,512]{1,0:T(8,128)} %collective-permute-done.5), channel_id=1, source_target_pairs={{2,0},{3,1},{4,6},{5,7},{10,8},{11,9},{12,14},{13,15},{18,16},{19,... | collective-permute-start | bytes 4718600 | tf_op jit(solution)/shard_map/ppermute | solution.py:189
  152.3 73.0 %collective-permute-start.15 = (f32[768,512]{1,0:T(8,128)}, f32[768,512]{1,0:T(8,128)}, u32[]{:S(2)}, u32[]{:S(2)}) collective-permute-start(f32[768,512]{1,0:T(8,128)} %add.93.refs_0_.refs_2_), channel_id=1, source_target_pairs={{1,0},{0,1},{3,2},{2,3},{5,4},{4,5},{7,6},{6,7},{9,8},{8,9},{11,10... | collective-permute-start | bytes 4718600 | tf_op jit(solution)/shard_map/ppermute | solution.py:189
  153.5 68.6 %collective-permute-start.11 = (f32[768,512]{1,0:T(8,128)}, f32[768,512]{1,0:T(8,128)S(1)}, u32[]{:S(2)}, u32[]{:S(2)}) collective-permute-start(f32[768,512]{1,0:T(8,128)} %collective-permute-done.6), channel_id=1, source_target_pairs={{2,0},{3,1},{4,6},{5,7},{10,8},{11,9},{12,14},{13,15},{18,16},{19,... | collective-permute-start | bytes 4718600 | tf_op jit(solution)/shard_map/ppermute | solution.py:189
  191.7 48.7 %collective-permute-start.18 = (f32[768,512]{1,0:T(8,128)}, f32[768,512]{1,0:T(8,128)}, u32[]{:S(2)}, u32[]{:S(2)}) collective-permute-start(f32[768,512]{1,0:T(8,128)} %add.96.refs_0_.refs_3_), channel_id=1, source_target_pairs={{1,0},{0,1},{3,2},{2,3},{5,4},{4,5},{7,6},{6,7},{9,8},{8,9},{11,10... | collective-permute-start | bytes 4718600 | tf_op jit(solution)/shard_map/ppermute | solution.py:189
  225.0 33.6 %collective-permute-start.16 = (f32[768,512]{1,0:T(8,128)}, f32[768,512]{1,0:T(8,128)}, u32[]{:S(2)}, u32[]{:S(2)}) collective-permute-start(f32[768,512]{1,0:T(8,128)} %add.99.refs_0_.refs_3_), channel_id=1, source_target_pairs={{1,0},{0,1},{3,2},{2,3},{5,4},{4,5},{7,6},{6,7},{9,8},{8,9},{11,10... | collective-permute-start | bytes 4718600 | tf_op jit(solution)/shard_map/ppermute | solution.py:189
  225.2 33.4 %collective-permute-start.14 = (f32[768,512]{1,0:T(8,128)}, f32[768,512]{1,0:T(8,128)}, u32[]{:S(2)}, u32[]{:S(2)}) collective-permute-start(f32[768,512]{1,0:T(8,128)} %collective-permute-done.10.refs_0_.refs_4_), channel_id=1, source_target_pairs={{2,0},{3,1},{0,2},{1,3},{6,4},{7,5},{4,6},{5,7},{10,8},{11,9},{8,1... | collective-permute-start | bytes 4718600 | tf_op jit(solution)/shard_map/ppermute | solution.py:189
  250.3 27.1 %collective-permute-start.19 = (f32[1536,512]{1,0:T(8,128)}, f32[1536,512]{1,0:T(8,128)}, u32[]{:S(2)}, u32[]{:S(2)}) collective-permute-start(f32[1536,512]{1,0:T(8,128)} %shard_map.77.refs_8_), channel_id=1, source_target_pairs={{0,8},{8,0},{1,9},{9,1},{2,10},{10,2},{3,11},{11,3},{4,12},{12,4},... | collective-permute-start | bytes 9437192 | tf_op jit(solution)/shard_map/ppermute | solution.py:272
  273.4 13.2 %collective-permute-start.17 = (f32[1536,512]{1,0:T(8,128)}, f32[1536,512]{1,0:T(8,128)}, u32[]{:S(2)}, u32[]{:S(2)}) collective-permute-start(f32[1536,512]{1,0:T(8,128)} %shard_map.76.refs_8_), channel_id=1, source_target_pairs={{0,8},{8,0},{1,9},{9,1},{2,10},{10,2},{3,11},{11,3},{4,12},{12,4},... | collective-permute-start | bytes 9437192 | tf_op jit(solution)/shard_map/ppermute | solution.py:272
  285.9 8.4 %collective-permute-start.20 = (f32[256,512]{1,0:T(8,128)S(1)}, f32[256,512]{1,0:T(8,128)S(1)}, u32[]{:S(2)}, u32[]{:S(2)}) collective-permute-start(f32[256,512]{1,0:T(8,128)S(1)} %slice_select_fusion.1), channel_id=1, source_target_pairs={{1,0},{0,1},{3,2},{2,3},{13,12},{12,13},{15,14},{14,15},{17,16},{1... | collective-permute-start | bytes 1572872 | tf_op jit(solution)/shard_map/ppermute | solution.py:255
  293.6 1.6 collective-permute-start.26
  294.5 1.6 collective-permute-start.21
  295.4 1.5 collective-permute-start.27
  296.2 1.5 collective-permute-start.22
  297.0 1.5 collective-permute-start.28
  297.8 1.5 collective-permute-start.23
  298.6 1.5 collective-permute-start.29
  299.4 1.5 collective-permute-start.24
  300.2 2.1 collective-permute-start.30
  301.0 49.3 %collective-permute-start.25 = (f32[512,512]{1,0:T(8,128)S(1)}, f32[512,512]{1,0:T(8,128)}, u32[]{:S(2)}, u32[]{:S(2)}) collective-permute-start(f32[512,512]{1,0:T(8,128)S(1)} %maximum_select_fusion), channel_id=1, source_target_pairs={{0,8},{1,9},{2,10},{3,11},{12,4},{13,5},{14,6},{15,7},{16,24},{17,... | collective-permute-start | bytes 3145736 | tf_op jit(solution)/shard_map/ppermute | solution.py:267
  302.5 55.5 %collective-permute-start.31 = (f32[512,512]{1,0:T(8,128)S(1)}, f32[512,512]{1,0:T(8,128)}, u32[]{:S(2)}, u32[]{:S(2)}) collective-permute-start(f32[512,512]{1,0:T(8,128)S(1)} %maximum_select_fusion.1), channel_id=1, source_target_pairs={{0,8},{1,9},{2,10},{3,11},{12,4},{13,5},{14,6},{15,7},{16,24},{17,... | collective-permute-start | bytes 3145736 | tf_op jit(solution)/shard_map/ppermute | solution.py:267
  (9 other events, 33.7 us)

commit v3 on v2

--- a/solution.py
+++ b/solution.py
@@ -12,71 +12,68 @@
 HIGHEST = lax.Precision.HIGHEST
 
 
-def _accumulate_body(n, row_step, ncols_blk, has_acc, tab, mask, *refs):
-    pieces, refs = refs[:n], refs[n:]
-    a_ref = refs[0]
-    acc_ref = refs[1] if has_acc else None
+def _accumulate_body(n, ncols_blk, has_acc, tab, mask, *refs):
+    pieces, tiles, refs = refs[:n], refs[n : 2 * n], refs[2 * n :]
+    acc_ref = refs[0] if has_acc else None
     out_ref, u_ref = refs[-2:]
     depth = pieces[0].shape[0]
-    t = pl.program_id(0)
-
-    @pl.when(t == 0)
+    rows = out_ref.shape[0]
+    m = pl.program_id(0)
+
+    @pl.when(m == 0)
     def _():
-        if has_acc:
-            out_ref[...] = acc_ref[...]
-        else:
-            out_ref[...] = jnp.zeros_like(out_ref)
-
-    for k, piece in enumerate(pieces):
-
-        @pl.when(t == k)
-        def _(piece=piece):
-            v = piece[...]
+        for k, piece in enumerate(pieces):
+            v, at = piece[...], 3 * k * depth
             hi = v.astype(jnp.bfloat16)
-            u_ref[0:depth, :] = hi
-            u_ref[depth : 2 * depth, :] = (v - hi.astype(jnp.float32)).astype(jnp.bfloat16)
-            u_ref[2 * depth : 3 * depth, :] = hi
+            u_ref[at : at + depth, :] = hi
+            u_ref[at + depth : at + 2 * depth, :] = (v - hi.astype(jnp.float32)).astype(
+                jnp.bfloat16
+            )
+            u_ref[at + 2 * depth : at + 3 * depth, :] = hi
 
     per = depth // BLK
-    col0 = tab[t] * per
     lane = lax.broadcasted_iota(jnp.int32, (1, depth), 1) // BLK
-    for m in range(a_ref.shape[0] // row_step):
-        rows = []
-        for b in range(row_step // BLK):
-            blk = m * (row_step // BLK) + b
+    lhs = []
+    for k, tile in enumerate(tiles):
+        col0 = tab[k] * per
+        kept = []
+        for b in range(rows // BLK):
+            row0 = (m * (rows // BLK) + b) * ncols_blk + col0
             keep = jnp.zeros((1, depth), jnp.float32)
             for j in range(per):
-                kept = mask[blk * ncols_blk + col0 + j].astype(jnp.float32)
-                keep = jnp.where(lane == j, kept, keep)
-            rows.append(a_ref[blk * BLK : (blk + 1) * BLK, :] * keep)
-        a = jnp.concatenate(rows, axis=0)
+                keep = jnp.where(lane == j, mask[row0 + j].astype(jnp.float32), keep)
+            kept.append(tile[b * BLK : (b + 1) * BLK, :] * keep)
+        a = jnp.concatenate(kept, axis=0)
         hi = a.astype(jnp.bfloat16)
         lo = (a - hi.astype(jnp.float32)).astype(jnp.bfloat16)
-        lhs = jnp.concatenate([hi, hi, lo], axis=1)
-        at = slice(m * row_step, (m + 1) * row_step)
-        out_ref[at, :] += jnp.dot(lhs, u_ref[...], preferred_element_type=jnp.float32)
+        lhs += [hi, hi, lo]
+    total = jnp.dot(
+        jnp.concatenate(lhs, axis=1), u_ref[...], preferred_element_type=jnp.float32
+    )
+    out_ref[...] = total + acc_ref[...] if has_acc else total
 
 
 def accumulate(acc, sigma, mask, table, pieces, light=1):
     nrows, ncols = sigma.shape
     depth, width = pieces[0].shape
     n = len(pieces)
-    row_step = next(s for s in (512, 256, 128) if nrows % s == 0)
-    whole = lambda shape: pl.BlockSpec(shape, lambda t, *_: (0, 0), pipeline_mode=pl.Buffered(1))
-    in_specs = [whole(p.shape) for p in pieces]
-    in_specs.append(pl.BlockSpec((nrows, depth), lambda t, tab, mask: (0, tab[t])))
-    args = [*pieces, sigma]
+    step = next(s for s in (256, 128) if nrows % s == 0)
+    whole = lambda shape: pl.BlockSpec(shape, lambda m, *_: (0, 0), pipeline_mode=pl.Buffered(1))
+    rows = pl.BlockSpec((step, width), lambda m, *_: (m, 0))
+    tile = lambda k: pl.BlockSpec((step, depth), lambda m, tab, mask: (m, tab[k]))
+    in_specs = [whole(p.shape) for p in pieces] + [tile(k) for k in range(n)]
+    args = [*pieces, *[sigma] * n]
     if acc is not None:
-        in_specs.append(whole(acc.shape))
+        in_specs.append(rows)
         args.append(acc)
     return pl.pallas_call(
-        functools.partial(_accumulate_body, n, row_step, ncols // BLK, acc is not None),
+        functools.partial(_accumulate_body, n, ncols // BLK, acc is not None),
         grid_spec=pltpu.PrefetchScalarGridSpec(
             num_scalar_prefetch=2,
-            grid=(n,),
+            grid=(nrows // step,),
             in_specs=in_specs,
-            out_specs=whole((nrows, width)),
-            scratch_shapes=[pltpu.VMEM((3 * depth, width), jnp.bfloat16)],
+            out_specs=rows,
+            scratch_shapes=[pltpu.VMEM((3 * n * depth, width), jnp.bfloat16)],
         ),
         out_shape=jax.ShapeDtypeStruct((nrows, width), jnp.float32),
         compiler_params=pltpu.CompilerParams(
@@ -214,42 +211,11 @@
         dims = (((0,), (0,)), ((), ()))
         return lax.dot_general(a, b, dims, precision=precision)
 
-    a0, b0 = lax.optimization_barrier((scale(0, 0, width), scale(1, 0, width)))
-    ax0, a1, am = recv(ox, a0), recv(za, a0), recv(inner, a0, mids)
-    b1, bx0 = recv(za, b0), recv(ox, b0)
-    acc_a = add(None, (near[0], a0))
-    acc_b = add(None, (near[0], b0))
-    bm = recv(inner, after(b0, am), mids)
-    square = jnp.stack([tdot(diag_inverse[i], diag_inverse[i], HIGHEST) for i in range(ns)])
-    a1, ax0, am, acc_a, acc_b, square = lax.optimization_barrier(
-        (a1, ax0, am, acc_a, acc_b, square)
-    )
-    ae, an, ax1 = recv(inner, am, ends), recv(inner, a1, mids), recv(ox, a1)
-    be, bn = recv(inner, bm, ends), recv(inner, b1, mids)
-    acc_a = add(acc_a, (far[0], ax0), (near[1], a1))
-    acc_b = add(acc_b, (far[0], bx0), (near[1], b1))
-    a2 = am + ae
-    ax2 = recv(ox, after(a2, acc_a, acc_b))
-    ax1, an, bn, a2, bm, be, acc_a, acc_b = lax.optimization_barrier(
-        (ax1, an, bn, a2, bm, be, acc_a, acc_b)
-    )
-    b2 = bm + be
-    af, bf, bx2 = recv(inner, an, ends), recv(inner, bn, ends), recv(ox, b2)
-    acc_b = add(acc_b, (near[2], after(b2, ax2)))
-    acc_a = add(acc_a, (far[1], after(ax1, ax2)), (near[2], a2))
-    a3 = an + af
-    ax3 = recv(ox, after(a3, acc_a, acc_b))
-    acc_a = add(acc_a, (near[3], a3), (far[2], ax2))
-    bf, bn, bx0, acc_a, acc_b = lax.optimization_barrier((bf, bn, bx0, acc_a, acc_b))
-    b3 = bn + bf
-    bx1, bx3 = recv(za, bx0), recv(ox, b3)
-    acc_b = add(acc_b, (near[3], b3), (far[2], bx2), light=1000)
-    acc_a = add(acc_a, (far[3], after(ax3, acc_b)), light=1000)
-
     own_r = lambda i: i // (ncol // 2)
     holder = lambda i: own_r(i) * ncol + i
     other = lambda i: (1 - own_r(i)) * ncol + i
     is_holder = r == c // (ncol // 2)
+
     def recv_holder(frm, v, who=every):
         pairs = [(holder(src), holder(dst)) for src, dst in mesh_pairs(frm, who)]
         return lax.ppermute(v, ("row", "col"), pairs)
@@ -271,13 +237,48 @@
     place = jnp.stack([x, pick])
     swap = lambda v: lax.ppermute(v, "row", [(0, 1), (1, 0)])
     shape = (ns, grid_rows, width)
+
+    a0, b0 = lax.optimization_barrier((scale(0, 0, width), scale(1, 0, width)))
+    ax0, a1, am = recv(ox, a0), recv(za, a0), recv(inner, a0, mids)
+    b1, bx0 = recv(za, b0), recv(ox, b0)
+    acc_a = add(None, (near[0], a0))
+    acc_b = add(None, (near[0], b0))
+    bm = recv(inner, after(b0, am), mids)
+    square = jnp.stack([tdot(diag_inverse[i], diag_inverse[i], HIGHEST) for i in range(ns)])
+    a1, ax0, am, acc_a, acc_b, square = lax.optimization_barrier(
+        (a1, ax0, am, acc_a, acc_b, square)
+    )
+    ae, an, ax1 = recv(inner, am, ends), recv(inner, a1, mids), recv(ox, a1)
+    bn = recv(inner, b1, mids)
+    af = recv(inner, an, ends)
+    acc_a = add(acc_a, (far[0], ax0), (near[1], a1))
+    acc_b = add(acc_b, (far[0], bx0), (near[1], b1))
+    a2 = am + ae
+    ax2 = recv(ox, after(a2, acc_a, acc_b))
+    ax1, an, af, bn, a2, bm, acc_a, acc_b = lax.optimization_barrier(
+        (ax1, an, af, bn, a2, bm, acc_a, acc_b)
+    )
+    a3 = an + af
+    ax3 = recv(ox, a3)
+    be, bf = recv(inner, bm, ends), recv(inner, bn, ends)
+    acc_a = add(
+        acc_a, (far[1], after(ax1, ax2)), (near[2], a2), (near[3], a3), (far[2], ax2), light=1000
+    )
+    b2 = after(bm + be, acc_a)
+    bx2 = recv(ox, b2)
+    acc_a = add(acc_a, (far[3], after(ax3, b2)), light=1000)
     got_a = swap(acc_a)
-    acc_b = add(acc_b, (far[1], bx1), (far[3], bx3))
-    got_b = swap(acc_b)
+    bf, bn, bx0, bx2, acc_a = lax.optimization_barrier((bf, bn, bx0, bx2, acc_a))
+    b3 = bn + bf
+    bx1, bx3 = recv(za, bx0), recv(ox, b3)
+    acc_b = add(acc_b, (near[2], b2), (near[3], b3), (far[2], bx2), light=1000)
     got_a = after(got_a, acc_b)
     full, term_a = finish(None, acc_a, got_a, place, (a0, a1, a2, a3), (ax0, ax1, ax2, ax3), shape, 0)
+    acc_b = add(acc_b, (far[1], bx1), (far[3], after(bx3, term_a)))
+    sum_a = total(term_a)
+    got_b = swap(acc_b)
     full, term_b = finish(full, acc_b, got_b, place, (b0, b1, b2, b3), (bx0, bx1, bx2, bx3), shape, 1)
-    return full, square - jnp.stack([total(term_a), total(term_b)])
+    return full, square - jnp.stack([sum_a, total(term_b)])
 
 
 def plain_path(sigma_anc, factor_rows, diag_inverse, row_pattern, anc_pattern):

time: 368 us -> 355 us (0.965); the launches traced: 362 us -> 353 us
  Pallas kernels: 134 us -> 119 us
  starting transfers between devices: 39.8 us -> 48.9 us
    pallas_call x10 -> x8, Pallas kernels: 121 us -> 105 us  [accumulate(): pl.pallas_call(functools.partial(_accumulate_body, n, ncols // BLK, acc i...]
    ppermute x18, starting transfers between devices: 22.4 us -> 28.2 us  [recv(): return lax.ppermute(v, 'col', mesh_pairs(frm, who))]
    ppermute x2, waiting for transfers between devices: 52.7 us -> 48.2 us  [total(): return jnp.where(is_holder, term, lax.ppermute(term, ('row', 'col'), pairs))]
    unnamed x20 -> x36, local copies, waits for them, and re-layouts: 7.94 us -> 9.17 us
  transfers between devices with their start and end apart: 32 -> 32, of which waited for: 10 -> 11; matrix products, arithmetic and copies ran while one was open for 7% -> 6% of each run, Pallas kernels for 37% -> 30%
where the time goes in v3:
time: 355 us; the launch traced here: 353 us
  waiting for transfers between devices  145 us (41%)
  Pallas kernels  119 us (34%)
  starting transfers between devices  48.9 us (14%)
  other arithmetic  20.8 us (6%)
  local copies, waits for them, and re-layouts  10 us (3%)
  matrix products  8.32 us (2%)
    pallas_call x8, Pallas kernels, accumulate(): pl.pallas_call(functools.partial(_accumulate_body, n, ncols // BLK, acc i...  105 us
    ppermute x18, waiting for transfers between devices, recv(): return lax.ppermute(v, 'col', mesh_pairs(frm, who))  93.8 us
    ppermute x2, waiting for transfers between devices, total(): return jnp.where(is_holder, term, lax.ppermute(term, ('row', 'col'), pairs))  48.2 us
    ppermute x18, starting transfers between devices, recv(): return lax.ppermute(v, 'col', mesh_pairs(frm, who))  28.2 us
    pallas_call x2, Pallas kernels, finish(): pl.pallas_call(functools.partial(_finish_body, len(near)), grid_spec=pltp...  13.9 us
    ppermute x2, starting transfers between devices, grid_path(): swap = lambda v: lax.ppermute(v, 'row', [(0, 1), (1, 0)])  10.8 us
    unnamed x36, local copies, waits for them, and re-layouts  9.17 us
    ppermute x10, starting transfers between devices, recv_holder(): return lax.ppermute(v, ('row', 'col'), pairs)  7.29 us
  transfers between devices with their start and end apart: 32, of which 11 were waited for; matrix products, arithmetic and copies ran while one was open for 6% of the time, Pallas kernels for 30%

profile of v3, /device:TPU:1, one launch (start us, length us, event | category | flops | bytes accessed | tf_op | source)
XLA Modules:
  0.0 353.4 jit_solution(15368000685016277194)
XLA Ops:
  1.5 2.3 broadcast_multiply_fusion
  7.0 1.9 collective-permute-start.3
  8.9 3.5 collective-permute-start.1
  14.8 3.5 %convolution_bitcast_fusion = f32[1,512,512]{2,1,0:T(8,128)S(1)} fusion(f32[2,512,512]{2,1,0:T(8,128)} %param.7), kind=kOutput, calls=%fused_computation.7 | convolution fusion | flops 1610612736 | bytes 2097152 | tf_op jit(solution)/shard_map/dot_general | solution.py:212
  18.4 1.9 convolution_bitcast_fusion.1
  21.7 7.5 %shard_map.68.refs_4_ = f32[1536,512]{1,0:T(8,128)S(1)} custom-call(s32[1]{0:T(128)} %bitcast.6.tab, s32[576]{0:T(1024)S(1)} %reshape.12.mask, f32[768,512]{1,0:T(8,128)S(1)} %fusion.1.refs_0_, f32[1536,6144]{1,0:T(8,128)} %refs_3_.7), custom_call_target="tpu_custom_call" | custom-call | flops 3623878656 | bytes 6291456 | tf_op jit(solution)/shard_map/pallas_call | solution.py:69
  30.9 7.5 %shard_map.69.refs_4_ = f32[1536,512]{1,0:T(8,128)S(1)} custom-call(s32[1]{0:T(128)} %bitcast.6.tab, s32[576]{0:T(1024)S(1)} %reshape.12.mask, f32[768,512]{1,0:T(8,128)S(1)} %fusion.refs_0_, f32[1536,6144]{1,0:T(8,128)} %refs_3_.7), custom_call_target="tpu_custom_call" | custom-call | flops 3623878656 | bytes 6291456 | tf_op jit(solution)/shard_map/pallas_call | solution.py:69
  40.0 6.3 %collective-permute-done.1.refs_1_ = f32[768,512]{1,0:T(8,128)} collective-permute-done((f32[768,512]{1,0:T(8,128)S(1)}, f32[768,512]{1,0:T(8,128)}, u32[]{:S(2)}, u32[]{:S(2)}) %collective-permute-start.1) | collective-permute-done | bytes 1572896 | tf_op jit(solution)/shard_map/ppermute | solution.py:186
  47.2 1.8 collective-permute-start.5
  51.6 28.5 %collective-permute-done.refs_1_ = f32[768,512]{1,0:T(8,128)} collective-permute-done((f32[768,512]{1,0:T(8,128)S(1)}, f32[768,512]{1,0:T(8,128)}, u32[]{:S(2)}, u32[]{:S(2)}) %collective-permute-start) | collective-permute-done | bytes 1572896 | tf_op jit(solution)/shard_map/ppermute | solution.py:186
  85.2 13.8 %shard_map.70.refs_8_ = f32[1536,512]{1,0:T(8,128)} custom-call(s32[2]{0:T(128)S(1)} %pad_add_fusion.1.tab, s32[576]{0:T(1024)S(1)} %reshape.12.mask, f32[768,512]{1,0:T(8,128)} %collective-permute-done.2.refs_0_.refs_4_, f32[768,512]{1,0:T(8,128)} %collective-permute-done.1.refs_1_, f32[1536,6144]{1,0:T(8,128)} %refs_3_.7, f32[1536,6144]{1,0:T(8,128)} %refs_3_.7, ...), custom_call_target="tpu_custom_call" | custom-call | flops 7247757312 | bytes 12582912 | tf_op jit(solution)/shard_map/pallas_call | solution.py:69
  99.0 13.8 %shard_map.71.refs_6_ = f32[1536,512]{1,0:T(8,128)} custom-call(s32[2]{0:T(128)S(1)} %pad_add_fusion.1.tab, s32[576]{0:T(1024)S(1)} %reshape.12.mask, f32[768,512]{1,0:T(8,128)} %collective-permute-done.10.refs_0_.refs_4_, f32[768,512]{1,0:T(8,128)} %collective-permute-done.refs_1_, f32[1536,6144]{1,0:T(8,128)} %refs_3_.7, f32[1536,6144]{1,0:T(8,128)} %refs_3_.7, ...), custom_call_target="tpu_custom_call" | custom-call | flops 7247757312 | bytes 12582912 | tf_op jit(solution)/shard_map/pallas_call | solution.py:69
  113.7 2.2 add.90.refs_1_.refs_2_
  117.3 30.2 %collective-permute-done.6 = f32[768,512]{1,0:T(8,128)} collective-permute-done((f32[768,512]{1,0:T(8,128)}, f32[768,512]{1,0:T(8,128)}, u32[]{:S(2)}, u32[]{:S(2)}) %collective-permute-start.6) | collective-permute-done | bytes 1572896 | tf_op jit(solution)/shard_map/ppermute | solution.py:186
  148.7 2.2 add.98.refs_2_.refs_3_
  153.6 21.8 %shard_map.72.refs_2_ = f32[1536,512]{1,0:T(8,128)} custom-call(s32[4]{0:T(128)S(1)} %pad_add_fusion.2.tab, s32[576]{0:T(1024)S(1)} %reshape.12.mask, f32[768,512]{1,0:T(8,128)} %collective-permute-done.4.refs_0_.refs_5_, f32[768,512]{1,0:T(8,128)S(1)} %add.90.refs_1_.refs_2_, f32[768,512]{1,0:T(8,128)S(1)} %add.98.refs_2_.refs_3_, ...), custom_call_target="tpu_custom_call" | custom-call | flops 14495514 | bytes 25165 | tf_op jit(solution)/shard_map/pallas_call | solution.py:69
  175.4 9.8 %collective-permute-done.11 = f32[768,512]{1,0:T(8,128)} collective-permute-done((f32[768,512]{1,0:T(8,128)}, f32[768,512]{1,0:T(8,128)}, u32[]{:S(2)}, u32[]{:S(2)}) %collective-permute-start.11) | collective-permute-done | bytes 1572896 | tf_op jit(solution)/shard_map/ppermute | solution.py:186
  185.2 2.2 add.93.refs_0_.refs_2_
  188.8 9.7 %shard_map.73.refs_8_ = f32[1536,512]{1,0:T(8,128)} custom-call(s32[1]{0:T(128)} %bitcast.15.tab, s32[576]{0:T(1024)S(1)} %reshape.12.mask, f32[768,512]{1,0:T(8,128)} %collective-permute-done.15.refs_0_.refs_7_, f32[1536,6144]{1,0:T(8,128)} %refs_3_.7, f32[1536,512]{1,0:T(8,128)} %shard_map.72.refs_2_), custom_call_target="tpu_custom_call" | custom-call | flops 3623878 | bytes 6291 | tf_op jit(solution)/shard_map/pallas_call | solution.py:69
  198.5 6.2 %collective-permute-start.18 = (f32[1536,512]{1,0:T(8,128)}, f32[1536,512]{1,0:T(8,128)}, u32[]{:S(2)}, u32[]{:S(2)}) collective-permute-start(f32[1536,512]{1,0:T(8,128)} %shard_map.73.refs_8_), channel_id=1, source_target_pairs={{0,8},{8,0},{1,9},{9,1},{2,10},{10,2},{3,11},{11,3},{4,12},{12,4},... | collective-permute-start | bytes 9437192 | tf_op jit(solution)/shard_map/ppermute | solution.py:238
  204.7 14.1 %collective-permute-done.13 = f32[768,512]{1,0:T(8,128)S(1)} collective-permute-done((f32[768,512]{1,0:T(8,128)}, f32[768,512]{1,0:T(8,128)S(1)}, u32[]{:S(2)}, u32[]{:S(2)}) %collective-permute-start.13) | collective-permute-done | bytes 1572896 | tf_op jit(solution)/shard_map/ppermute | solution.py:186
  218.8 3.5 add.100.refs_1_.refs_3_
  223.6 4.1 %collective-permute-start.16 = (f32[768,512]{1,0:T(8,128)}, f32[768,512]{1,0:T(8,128)}, u32[]{:S(2)}, u32[]{:S(2)}) collective-permute-start(f32[768,512]{1,0:T(8,128)} %collective-permute-done.10.refs_0_.refs_4_), channel_id=1, source_target_pairs={{2,0},{3,1},{0,2},{1,3},{6,4},{7,5},{4,6},{5,7},{10,8},{11,9},{8,1... | collective-permute-start | bytes 4718600 | tf_op jit(solution)/shard_map/ppermute | solution.py:186
  230.7 16.9 %shard_map.74.refs_4_ = f32[1536,512]{1,0:T(8,128)} custom-call(s32[3]{0:T(128)S(1)} %pad_add_fusion.4.tab, s32[576]{0:T(1024)S(1)} %reshape.12.mask, f32[768,512]{1,0:T(8,128)S(1)} %copy-done.1, f32[768,512]{1,0:T(8,128)} %add.100.refs_1_.refs_3_, f32[768,512]{1,0:T(8,128)S(1)} %copy-done.10, f32[1536,6144]{1,0:T(8,128)} %refs_3_.7, f32[1536,6144]{1,0:T(8,128)} %refs_3_.7, ...), custom_call_target="tpu_custom_call" | custom-call | flops 10871635 | bytes 18874 | tf_op jit(solution)/shard_map/pallas_call | solution.py:69
  247.6 6.9 %shard_map.75 = (f32[2,1536,512]{2,1,0:T(8,128)}, f32[512,512]{1,0:T(8,128)S(1)}) custom-call(s32[2]{0:T(128)S(1)} %pad_add_fusion.place, f32[768,512]{1,0:T(8,128)S(1)} %copy-done.6, f32[768,512]{1,0:T(8,128)} %collective-permute-done.1.refs_1_, f32[768,512]{1,0:T(8,128)S(1)} %add.90.refs_1_.refs_2_, f32[768,512]{1,0:T(8,128)S(1)} %add.98.refs_2_.refs_3_, ...), custom_call_target="tpu_custom_call" | custom-call | flops 393216 | bytes 393216 | tf_op jit(solution)/shard_map/pallas_call | solution.py:140
  255.6 3.1 collective-permute-done.16.refs_0_.refs_5_
  258.7 13.8 %shard_map.76.refs_8_ = f32[1536,512]{1,0:T(8,128)} custom-call(s32[2]{0:T(128)S(1)} %pad_add_fusion.3.tab, s32[576]{0:T(1024)S(1)} %reshape.12.mask, f32[768,512]{1,0:T(8,128)} %collective-permute-done.16.refs_0_.refs_5_, f32[768,512]{1,0:T(8,128)} %collective-permute-done.17.refs_1_.refs_7_, f32[1536,6144]{1,0:T(8,128)} %refs_3_.7, f32[1536,6144]{1,0:T(8,128)} %refs_3_.7, ...), custom_call_target="tpu_custom_call" | custom-call | flops 7247757312 | bytes 12582912 | tf_op jit(solution)/shard_map/pallas_call | solution.py:69
  272.4 4.7 %collective-permute-start.19 = (f32[1536,512]{1,0:T(8,128)}, f32[1536,512]{1,0:T(8,128)}, u32[]{:S(2)}, u32[]{:S(2)}) collective-permute-start(f32[1536,512]{1,0:T(8,128)} %shard_map.76.refs_8_), channel_id=1, source_target_pairs={{0,8},{8,0},{1,9},{9,1},{2,10},{10,2},{3,11},{11,3},{4,12},{12,4},... | collective-permute-start | bytes 9437192 | tf_op jit(solution)/shard_map/ppermute | solution.py:238
  279.3 3.4 collective-permute-done.19.refs_9_
  284.2 6.9 %shard_map.77 = (f32[2,1536,512]{2,1,0:T(8,128)}, f32[512,512]{1,0:T(8,128)S(1)}) custom-call(s32[2]{0:T(128)S(1)} %pad_add_fusion.place, f32[768,512]{1,0:T(8,128)S(1)} %copy-done.4, f32[768,512]{1,0:T(8,128)} %collective-permute-done.refs_1_, f32[768,512]{1,0:T(8,128)S(1)} %copy-done.2, ...), custom_call_target="tpu_custom_call", output_to_operand_aliasing={{0}: (11, {})} | custom-call | flops 393216 | bytes 393216 | tf_op jit(solution)/shard_map/pallas_call | solution.py:140
  301.7 41.4 %collective-permute-done.25 = f32[512,512]{1,0:T(8,128)S(1)} collective-permute-done((f32[512,512]{1,0:T(8,128)S(1)}, f32[512,512]{1,0:T(8,128)S(1)}, u32[]{:S(2)}, u32[]{:S(2)}) %collective-permute-start.25) | collective-permute-done | bytes 1048608 | tf_op jit(solution)/shard_map/ppermute | solution.py:233
  343.4 6.7 %collective-permute-done.31 = f32[512,512]{1,0:T(8,128)} collective-permute-done((f32[512,512]{1,0:T(8,128)S(1)}, f32[512,512]{1,0:T(8,128)}, u32[]{:S(2)}, u32[]{:S(2)}) %collective-permute-start.31) | collective-permute-done | bytes 1048608 | tf_op jit(solution)/shard_map/ppermute | solution.py:233
  (112 shorter events, 49.9 us)
Async XLA Ops:
  7.0 33.0 %collective-permute-start.3 = (f32[768,512]{1,0:T(8,128)S(1)}, f32[768,512]{1,0:T(8,128)}, u32[]{:S(2)}, u32[]{:S(2)}) collective-permute-start(f32[768,512]{1,0:T(8,128)S(1)} %fusion.1.refs_0_), channel_id=1, source_target_pairs={{4,2},{5,3},{2,4},{3,5},{12,10},{13,11},{10,12},{11,13},{20,18},{2... | collective-permute-start | bytes 4718600 | tf_op jit(solution)/shard_map/ppermute | solution.py:186
  8.9 37.4 %collective-permute-start.1 = (f32[768,512]{1,0:T(8,128)S(1)}, f32[768,512]{1,0:T(8,128)}, u32[]{:S(2)}, u32[]{:S(2)}) collective-permute-start(f32[768,512]{1,0:T(8,128)S(1)} %fusion.1.refs_0_), channel_id=1, source_target_pairs={{2,0},{3,1},{0,2},{1,3},{6,4},{7,5},{4,6},{5,7},{10,8},{11,9},{8,1... | collective-permute-start | bytes 4718600 | tf_op jit(solution)/shard_map/ppermute | solution.py:186
  12.4 34.7 %collective-permute-start.2 = (f32[768,512]{1,0:T(8,128)S(1)}, f32[768,512]{1,0:T(8,128)}, u32[]{:S(2)}, u32[]{:S(2)}) collective-permute-start(f32[768,512]{1,0:T(8,128)S(1)} %fusion.1.refs_0_), channel_id=1, source_target_pairs={{1,0},{0,1},{3,2},{2,3},{5,4},{4,5},{7,6},{6,7},{9,8},{8,9},{11,10... | collective-permute-start | bytes 4718600 | tf_op jit(solution)/shard_map/ppermute | solution.py:186
  13.6 66.4 %collective-permute-start = (f32[768,512]{1,0:T(8,128)S(1)}, f32[768,512]{1,0:T(8,128)}, u32[]{:S(2)}, u32[]{:S(2)}) collective-permute-start(f32[768,512]{1,0:T(8,128)S(1)} %fusion.refs_0_), channel_id=1, source_target_pairs={{2,0},{3,1},{0,2},{1,3},{6,4},{7,5},{4,6},{5,7},{10,8},{11,9},{8,1... | collective-permute-start | bytes 4718600 | tf_op jit(solution)/shard_map/ppermute | solution.py:186
  13.7 68.1 %collective-permute-start.10 = (f32[768,512]{1,0:T(8,128)S(1)}, f32[768,512]{1,0:T(8,128)}, u32[]{:S(2)}, u32[]{:S(2)}) collective-permute-start(f32[768,512]{1,0:T(8,128)S(1)} %fusion.refs_0_), channel_id=1, source_target_pairs={{1,0},{0,1},{3,2},{2,3},{5,4},{4,5},{7,6},{6,7},{9,8},{8,9},{11,10... | collective-permute-start | bytes 4718600 | tf_op jit(solution)/shard_map/ppermute | solution.py:186
  47.2 36.5 %collective-permute-start.5 = (f32[768,512]{1,0:T(8,128)}, f32[768,512]{1,0:T(8,128)}, u32[]{:S(2)}, u32[]{:S(2)}) collective-permute-start(f32[768,512]{1,0:T(8,128)} %collective-permute-done.1.refs_1_), channel_id=1, source_target_pairs={{4,2},{5,3},{2,4},{3,5},{12,10},{13,11},{10,12},{11,13},{20,18},{2... | collective-permute-start | bytes 4718600 | tf_op jit(solution)/shard_map/ppermute | solution.py:186
  49.0 64.7 %collective-permute-start.8 = (f32[768,512]{1,0:T(8,128)}, f32[768,512]{1,0:T(8,128)}, u32[]{:S(2)}, u32[]{:S(2)}) collective-permute-start(f32[768,512]{1,0:T(8,128)} %collective-permute-done.3), channel_id=1, source_target_pairs={{2,0},{3,1},{4,6},{5,7},{10,8},{11,9},{12,14},{13,15},{18,16},{19,... | collective-permute-start | bytes 4718600 | tf_op jit(solution)/shard_map/ppermute | solution.py:186
  50.3 67.0 %collective-permute-start.4 = (f32[768,512]{1,0:T(8,128)}, f32[768,512]{1,0:T(8,128)}, u32[]{:S(2)}, u32[]{:S(2)}) collective-permute-start(f32[768,512]{1,0:T(8,128)} %collective-permute-done.1.refs_1_), channel_id=1, source_target_pairs={{1,0},{0,1},{3,2},{2,3},{5,4},{4,5},{7,6},{6,7},{9,8},{8,9},{11,10... | collective-permute-start | bytes 4718600 | tf_op jit(solution)/shard_map/ppermute | solution.py:186
  80.0 37.2 %collective-permute-start.9 = (f32[768,512]{1,0:T(8,128)S(1)}, f32[768,512]{1,0:T(8,128)}, u32[]{:S(2)}, u32[]{:S(2)}) collective-permute-start(f32[768,512]{1,0:T(8,128)S(1)} %fusion.refs_0_), channel_id=1, source_target_pairs={{4,2},{5,3},{2,4},{3,5},{12,10},{13,11},{10,12},{11,13},{20,18},{2... | collective-permute-start | bytes 4718600 | tf_op jit(solution)/shard_map/ppermute | solution.py:186
  81.8 35.4 %collective-permute-start.7 = (f32[768,512]{1,0:T(8,128)}, f32[768,512]{1,0:T(8,128)}, u32[]{:S(2)}, u32[]{:S(2)}) collective-permute-start(f32[768,512]{1,0:T(8,128)} %collective-permute-done.refs_1_), channel_id=1, source_target_pairs={{4,2},{5,3},{2,4},{3,5},{12,10},{13,11},{10,12},{11,13},{20,18},{2... | collective-permute-start | bytes 4718600 | tf_op jit(solution)/shard_map/ppermute | solution.py:186
  83.6 63.8 %collective-permute-start.6 = (f32[768,512]{1,0:T(8,128)}, f32[768,512]{1,0:T(8,128)}, u32[]{:S(2)}, u32[]{:S(2)}) collective-permute-start(f32[768,512]{1,0:T(8,128)} %collective-permute-done.5), channel_id=1, source_target_pairs={{2,0},{3,1},{4,6},{5,7},{10,8},{11,9},{12,14},{13,15},{18,16},{19,... | collective-permute-start | bytes 4718600 | tf_op jit(solution)/shard_map/ppermute | solution.py:186
  116.0 36.4 %collective-permute-start.12 = (f32[768,512]{1,0:T(8,128)S(1)}, f32[768,512]{1,0:T(8,128)}, u32[]{:S(2)}, u32[]{:S(2)}) collective-permute-start(f32[768,512]{1,0:T(8,128)S(1)} %add.90.refs_1_.refs_2_), channel_id=1, source_target_pairs={{1,0},{0,1},{3,2},{2,3},{5,4},{4,5},{7,6},{6,7},{9,8},{8,9},{11,10... | collective-permute-start | bytes 4718600 | tf_op jit(solution)/shard_map/ppermute | solution.py:186
  147.4 37.8 %collective-permute-start.11 = (f32[768,512]{1,0:T(8,128)}, f32[768,512]{1,0:T(8,128)}, u32[]{:S(2)}, u32[]{:S(2)}) collective-permute-start(f32[768,512]{1,0:T(8,128)} %collective-permute-done.9), channel_id=1, source_target_pairs={{2,0},{3,1},{4,6},{5,7},{10,8},{11,9},{12,14},{13,15},{18,16},{19,... | collective-permute-start | bytes 4718600 | tf_op jit(solution)/shard_map/ppermute | solution.py:186
  151.0 37.8 %collective-permute-start.15 = (f32[768,512]{1,0:T(8,128)S(1)}, f32[768,512]{1,0:T(8,128)}, u32[]{:S(2)}, u32[]{:S(2)}) collective-permute-start(f32[768,512]{1,0:T(8,128)S(1)} %add.98.refs_2_.refs_3_), channel_id=1, source_target_pairs={{1,0},{0,1},{3,2},{2,3},{5,4},{4,5},{7,6},{6,7},{9,8},{8,9},{11,10... | collective-permute-start | bytes 4718600 | tf_op jit(solution)/shard_map/ppermute | solution.py:186
  152.3 66.5 %collective-permute-start.13 = (f32[768,512]{1,0:T(8,128)}, f32[768,512]{1,0:T(8,128)S(1)}, u32[]{:S(2)}, u32[]{:S(2)}) collective-permute-start(f32[768,512]{1,0:T(8,128)} %collective-permute-done.7), channel_id=1, source_target_pairs={{2,0},{3,1},{4,6},{5,7},{10,8},{11,9},{12,14},{13,15},{18,16},{19,... | collective-permute-start | bytes 4718600 | tf_op jit(solution)/shard_map/ppermute | solution.py:186
  187.5 31.4 %collective-permute-start.14 = (f32[768,512]{1,0:T(8,128)S(1)}, f32[768,512]{1,0:T(8,128)S(1)}, u32[]{:S(2)}, u32[]{:S(2)}) collective-permute-start(f32[768,512]{1,0:T(8,128)S(1)} %add.93.refs_0_.refs_2_), channel_id=1, source_target_pairs={{1,0},{0,1},{3,2},{2,3},{5,4},{4,5},{7,6},{6,7},{9,8},{8,9},{11,10... | collective-permute-start | bytes 4718600 | tf_op jit(solution)/shard_map/ppermute | solution.py:186
  198.5 49.1 %collective-permute-start.18 = (f32[1536,512]{1,0:T(8,128)}, f32[1536,512]{1,0:T(8,128)}, u32[]{:S(2)}, u32[]{:S(2)}) collective-permute-start(f32[1536,512]{1,0:T(8,128)} %shard_map.73.refs_8_), channel_id=1, source_target_pairs={{0,8},{8,0},{1,9},{9,1},{2,10},{10,2},{3,11},{11,3},{4,12},{12,4},... | collective-permute-start | bytes 9437192 | tf_op jit(solution)/shard_map/ppermute | solution.py:238
  222.3 33.2 %collective-permute-start.17 = (f32[768,512]{1,0:T(8,128)}, f32[768,512]{1,0:T(8,128)}, u32[]{:S(2)}, u32[]{:S(2)}) collective-permute-start(f32[768,512]{1,0:T(8,128)} %add.100.refs_1_.refs_3_), channel_id=1, source_target_pairs={{1,0},{0,1},{3,2},{2,3},{5,4},{4,5},{7,6},{6,7},{9,8},{8,9},{11,10... | collective-permute-start | bytes 4718600 | tf_op jit(solution)/shard_map/ppermute | solution.py:186
  223.6 35.1 %collective-permute-start.16 = (f32[768,512]{1,0:T(8,128)}, f32[768,512]{1,0:T(8,128)}, u32[]{:S(2)}, u32[]{:S(2)}) collective-permute-start(f32[768,512]{1,0:T(8,128)} %collective-permute-done.10.refs_0_.refs_4_), channel_id=1, source_target_pairs={{2,0},{3,1},{0,2},{1,3},{6,4},{7,5},{4,6},{5,7},{10,8},{11,9},{8,1... | collective-permute-start | bytes 4718600 | tf_op jit(solution)/shard_map/ppermute | solution.py:186
  272.4 10.3 %collective-permute-start.19 = (f32[1536,512]{1,0:T(8,128)}, f32[1536,512]{1,0:T(8,128)}, u32[]{:S(2)}, u32[]{:S(2)}) collective-permute-start(f32[1536,512]{1,0:T(8,128)} %shard_map.76.refs_8_), channel_id=1, source_target_pairs={{0,8},{8,0},{1,9},{9,1},{2,10},{10,2},{3,11},{11,3},{4,12},{12,4},... | collective-permute-start | bytes 9437192 | tf_op jit(solution)/shard_map/ppermute | solution.py:238
  278.4 13.6 %collective-permute-start.20 = (f32[256,512]{1,0:T(8,128)S(1)}, f32[256,512]{1,0:T(8,128)S(1)}, u32[]{:S(2)}, u32[]{:S(2)}) collective-permute-start(f32[256,512]{1,0:T(8,128)S(1)} %slice_select_fusion.1), channel_id=1, source_target_pairs={{1,0},{0,1},{3,2},{2,3},{13,12},{12,13},{15,14},{14,15},{17,16},{1... | collective-permute-start | bytes 1572872 | tf_op jit(solution)/shard_map/ppermute | solution.py:221
  291.2 2.0 collective-permute-start.26
  292.5 1.6 collective-permute-start.21
  293.3 1.5 collective-permute-start.27
  294.1 1.5 collective-permute-start.22
  294.9 1.5 collective-permute-start.28
  295.7 1.5 collective-permute-start.23
  296.5 1.5 collective-permute-start.29
  297.3 1.5 collective-permute-start.24
  298.1 2.1 collective-permute-start.30
  299.0 44.2 %collective-permute-start.25 = (f32[512,512]{1,0:T(8,128)S(1)}, f32[512,512]{1,0:T(8,128)S(1)}, u32[]{:S(2)}, u32[]{:S(2)}) collective-permute-start(f32[512,512]{1,0:T(8,128)S(1)} %maximum_select_fusion), channel_id=1, source_target_pairs={{0,8},{1,9},{2,10},{3,11},{12,4},{13,5},{14,6},{15,7},{16,24},{17,... | collective-permute-start | bytes 3145736 | tf_op jit(solution)/shard_map/ppermute | solution.py:233
  300.4 49.7 %collective-permute-start.31 = (f32[512,512]{1,0:T(8,128)S(1)}, f32[512,512]{1,0:T(8,128)}, u32[]{:S(2)}, u32[]{:S(2)}) collective-permute-start(f32[512,512]{1,0:T(8,128)S(1)} %maximum_select_fusion.1), channel_id=1, source_target_pairs={{0,8},{1,9},{2,10},{3,11},{12,4},{13,5},{14,6},{15,7},{16,24},{17,... | collective-permute-start | bytes 3145736 | tf_op jit(solution)/shard_map/ppermute | solution.py:233
  (17 other events, 179.1 us)
